TPU v7x, 32 devices: a whole 2x2x4 slice. The times are simulated.
32 devices in a mesh: space: 16 (over z, y, core), chaos: 2 (over x).
Axes of the slice: x: 2, y: 2, z: 4, core: 2. Of those that a mesh axis runs over, the one named last changes fastest.
Arguments:
- right_side: float32 [168, 8192], P('chaos', 'space'), may hold values from -8 to 8, as said below
- diagonal: float32 [168, 8192], P('chaos', 'space'), may hold values from 1.5 to 4
- stiffness: float32 [9, 128, 64, 256], P(None, 'space'), may hold values from -0.015625 to 0.015625
- columns: int32 [128, 4], P('space'), may hold values from 0 to 9, as said below
- interface: int32 [16, 2], P('space'), may hold values from 0 to 7
- triples: int32 [885, 3], replicated, may hold values from 0 to 164, as said below
- coupling_values: float32 [885], replicated, may hold values from -1 to 1, as said below
Outputs:
- solution_field: float32 [168, 8192], P('chaos', 'space')
- residual: float32 [168, 8192], P('chaos', 'space')
Inputs may be any that keep to these rules, and one draw needn't show every extreme that they name: `right_side`: mode slots 165 and beyond are zero in every row. `columns`: entry 0 of block row b is b mod 8. Values below 8 name the partition's own block rows, 8 to 8 the blocks received from the previous partition, the rest those from the next. `triples`: no triple repeats. Term 0 holds (0, i, i) once for every mode i below 165. Every other entry has a term t of 1 to 8 and comes with its mirror (t, j, i), i != j; each mode is the row mode of at most two entries of one such term. `coupling_values`: an entry and its mirror carry equal values, so every coupling[t] is symmetric.
All inputs are finite; a program needn't handle non-finite values.
Results may differ from a plain program's by a relative error of at most 0.0003.
Values sent between devices are 32-bit elements; how exact they have to be, the bound alone decides.
A program may use at most 64 MiB of HBM per device.

v0:
```python
import jax
import jax.numpy as jnp
from jax import lax
from jax.sharding import PartitionSpec as P

MODE_SLOTS = 168
TERMS = 9
BLOCK = 64
IFACE = 1
ITERS = 3


def with_halo(cells, sides, width):
    for axis, dim in sides:
        count = lax.axis_size(axis)
        ends = count - 1
        head = lax.slice_in_dim(cells, 0, width, axis=dim)
        tail = lax.slice_in_dim(cells, cells.shape[dim] - width, cells.shape[dim], axis=dim)
        cells = jnp.concatenate(
            [
                lax.ppermute(tail, axis, [(i, (i + 1) % count) for i in range(ends)]),
                cells,
                lax.ppermute(head, axis, [((i + 1) % count, i) for i in range(ends)]),
            ],
            axis=dim,
        )
    return cells


def coupling_table(triples, coupling_values):
    row_keys = triples[:, 0] * MODE_SLOTS + triples[:, 1]
    row_hot = (
        row_keys[:, None] == jnp.arange(TERMS * MODE_SLOTS, dtype=jnp.int32)[None, :]
    ).astype(jnp.float32)
    row_hot = row_hot * coupling_values[:, None]
    col_hot = (triples[:, 2][:, None] == jnp.arange(MODE_SLOTS, dtype=jnp.int32)[None, :]).astype(
        jnp.float32
    )
    table = jnp.einsum("nk,nj->kj", row_hot, col_hot, precision=lax.Precision.HIGHEST)
    return table.reshape(TERMS, MODE_SLOTS, MODE_SLOTS)


def spatial_terms(vector, stiffness, columns, interface):
    mode_count, row_count = vector.shape
    block_rows, stored = columns.shape
    blocks = vector.reshape(mode_count, block_rows, BLOCK)
    packed = blocks[:, interface[0], :].reshape(mode_count, 2 * IFACE * BLOCK)
    widened = with_halo(packed, (("space", 1),), IFACE * BLOCK)
    from_left = widened[:, : IFACE * BLOCK].reshape(mode_count, IFACE, BLOCK)
    from_right = widened[:, widened.shape[1] - IFACE * BLOCK :].reshape(mode_count, IFACE, BLOCK)
    extended = jnp.concatenate([blocks, from_left, from_right], 1)
    picked = extended[:, columns.reshape(-1), :].reshape(mode_count, block_rows, stored * BLOCK)
    spatial = jnp.einsum("mbk,tbck->tmbc", picked, stiffness, precision=lax.Precision.HIGHEST)
    return spatial.reshape(TERMS, mode_count, row_count)


def apply_operator(vector, diagonal, stiffness, columns, interface, coupling):
    spatial = spatial_terms(vector, stiffness, columns, interface)
    mode_count = vector.shape[0]
    offset = lax.axis_index("chaos") * mode_count
    local_cols = lax.dynamic_slice_in_dim(coupling, offset, mode_count, 2)
    coupled = lax.psum_scatter(
        jnp.einsum("tij,tjr->ir", local_cols, spatial, precision=lax.Precision.HIGHEST),
        "chaos",
        scatter_dimension=0,
        tiled=True,
    )
    return diagonal * vector + coupled


def squares(residual):
    return lax.psum(jnp.sum(residual * residual), ("space", "chaos"))


def per_device(right_side, diagonal, stiffness, columns, interface, triples, coupling_values):
    coupling = coupling_table(triples, coupling_values)
    solution_field = jnp.zeros_like(right_side)
    residual = right_side
    direction = right_side
    norm_now = squares(residual)
    for iteration in range(ITERS):
        applied = apply_operator(direction, diagonal, stiffness, columns, interface, coupling)
        step_size = norm_now / lax.psum(jnp.sum(direction * applied), ("space", "chaos"))
        solution_field = solution_field + step_size * direction
        residual = residual - step_size * applied
        norm_next = squares(residual)
        direction = residual + norm_next / norm_now * direction
        norm_now = norm_next
    return (solution_field, residual)


def solution(mesh):
    placed = (
        P("chaos", "space"),
        P("chaos", "space"),
        P(None, "space", None, None),
        P("space", None),
        P("space", None),
        P(),
        P(),
    )
    return jax.shard_map(
        per_device,
        mesh=mesh,
        in_specs=placed,
        out_specs=(P("chaos", "space"), P("chaos", "space")),
        check_vma=False,
    )
```

profile of v0, /device:TPU:0, one launch (start us, length us, event | category | flops | bytes accessed | tf_op | source)
XLA Modules:
  0.0 319.3 jit_solution(13375855057861601399)
XLA Ops:
  1.3 1.0 copy.63
  2.9 2.4 collective-permute-start
  5.3 1.3 collective-permute-start.1
  6.6 0.8 copy.64
  7.4 0.9 slice_reduce_fusion
  8.3 5.6 %fusion.3 = f32[1512,168]{1,0:T(8,128)S(1)} fusion(f32[885]{0:T(1024)} %param.13, s32[885]{0:T(1024)S(1)} %get-tuple-element.7, s32[885]{0:T(1024)S(1)} %get-tuple-element.6), kind=kOutput, calls=%fused_computation.6 | convolution fusion | flops 2700474624 | bytes 1026684 | tf_op jit(solution)/shard_map/nk,nj->kj/dot_general | solution.py:39
  14.6 5.9 %fusion.14 = f32[9,84,8,64]{1,3,0,2:T(8,128)S(1)} fusion(f32[84,8,256,1]{0,2,3,1:T(8,128)S(1)} %bitcast.78, f32[9,8,64,256]{3,2,1,0:T(8,128)} %param.9), kind=kOutput, calls=%fused_computation.18 | convolution fusion | flops 1189085184 | bytes 6955008 | tf_op jit(solution)/shard_map/mbk,tbck->tmbc/dot_general | solution.py:53
  20.8 2.6 convolution_bitcast_fusion.2
  23.4 10.2 %fusion = f32[88,512]{1,0:T(8,128)S(1)} fusion(f32[168,512]{1,0:T(8,128)S(1)} %convolution_bitcast_fusion.2), kind=kCustom, calls=%all-reduce-scatter | all-reduce-scatter fusion | flops 90113 | bytes 524800
  33.6 1.5 collective-permute-start.6
  37.3 44.9 %all-reduce.6 = (f32[]{:T(128)}, f32[]{:T(128)}) all-reduce(f32[]{:T(128)} %get-tuple-element.5, f32[]{:T(128)} %get-tuple-element.4), channel_id=1, replica_groups=mesh['space'=16,'chaos'=2] {'space','chaos'}, use_global_device_ids=true, to_apply=%region_1.0 | all-reduce | flops 2 | bytes 16 | tf_op jit(solution)/shard_map/psum | solution.py:72
  84.2 40.9 %psum.44 = f32[]{:T(128)} all-reduce(f32[]{:T(128)} %get-tuple-element.12), channel_id=1, replica_groups=mesh['space'=16,'chaos'=2] {'space','chaos'}, use_global_device_ids=true, to_apply=%region_6.0 | all-reduce | flops 1 | bytes 8 | tf_op jit(solution)/shard_map/psum | solution.py:72
  127.2 1.3 collective-permute-start.2
  128.5 1.3 collective-permute-start.3
  129.8 4.6 %collective-permute-done.3 = f32[84,64]{0,1:T(8,128)S(1)} collective-permute-done((f32[84,64]{0,1:T(8,128)S(1)}, f32[84,64]{0,1:T(8,128)S(1)}, u32[]{:S(2)}, u32[]{:S(2)}) %collective-permute-start.3) | collective-permute-done | bytes 21536 | tf_op jit(solution)/shard_map/ppermute | solution.py:23
  135.1 5.9 %fusion.17 = f32[9,84,8,64]{1,3,0,2:T(8,128)S(1)} fusion(f32[84,8,256,1]{0,2,3,1:T(8,128)S(1)} %bitcast.79, f32[9,8,64,256]{3,2,1,0:T(8,128)} %param.9), kind=kOutput, calls=%fused_computation.19 | convolution fusion | flops 1189085184 | bytes 6955008 | tf_op jit(solution)/shard_map/mbk,tbck->tmbc/dot_general | solution.py:53
  141.2 2.6 convolution_bitcast_fusion.1
  143.8 8.3 %fusion.1 = f32[88,512]{1,0:T(8,128)S(1)} fusion(f32[168,512]{1,0:T(8,128)S(1)} %convolution_bitcast_fusion.1), kind=kCustom, calls=%all-reduce-scatter.1 | all-reduce-scatter fusion | flops 90113 | bytes 524800
  152.1 3.3 %collective-permute-start.7 = (f32[4,512]{1,0:T(4,128)S(1)}, f32[4,512]{1,0:T(4,128)S(1)}, u32[]{:S(2)}, u32[]{:S(2)}) collective-permute-start(f32[4,512]{1,0:T(4,128)S(1)} %slice.55), channel_id=1, source_target_pairs={{0,1},{2,3},{4,5},{6,7},{8,9},{10,11},{12,13},{14,15},{16,17},{18,... | collective-permute-start | bytes 24584
  155.4 1.3 collective-permute-done.7
  157.6 42.3 %psum.45 = f32[]{:T(128)} all-reduce(f32[]{:T(128)} %multiply_reduce_fusion.2), channel_id=1, replica_groups=mesh['space'=16,'chaos'=2] {'space','chaos'}, use_global_device_ids=true, to_apply=%region_9.0 | all-reduce | flops 1 | bytes 8 | tf_op jit(solution)/shard_map/psum | solution.py:83
  201.9 40.6 %psum.46 = f32[]{:T(128)} all-reduce(f32[]{:T(128)} %get-tuple-element.10), channel_id=1, replica_groups=mesh['space'=16,'chaos'=2] {'space','chaos'}, use_global_device_ids=true, to_apply=%region_11.0 | all-reduce | flops 1 | bytes 8 | tf_op jit(solution)/shard_map/psum | solution.py:72
  244.6 1.3 collective-permute-start.4
  245.9 1.3 collective-permute-start.5
  247.2 4.5 %collective-permute-done.5 = f32[84,64]{0,1:T(8,128)S(1)} collective-permute-done((f32[84,64]{0,1:T(8,128)S(1)}, f32[84,64]{0,1:T(8,128)S(1)}, u32[]{:S(2)}, u32[]{:S(2)}) %collective-permute-start.5) | collective-permute-done | bytes 21536 | tf_op jit(solution)/shard_map/ppermute | solution.py:23
  252.4 5.9 %fusion.20 = f32[9,84,8,64]{1,3,0,2:T(8,128)S(1)} fusion(f32[84,8,256,1]{0,2,3,1:T(8,128)S(1)} %bitcast.77, f32[9,8,64,256]{3,2,1,0:T(8,128)} %param.9), kind=kOutput, calls=%fused_computation.20 | convolution fusion | flops 1189085184 | bytes 6955008 | tf_op jit(solution)/shard_map/mbk,tbck->tmbc/dot_general | solution.py:53
  258.5 2.6 convolution_bitcast_fusion
  261.1 9.1 %fusion.2 = f32[88,512]{1,0:T(8,128)S(1)} fusion(f32[168,512]{1,0:T(8,128)S(1)} %convolution_bitcast_fusion), kind=kCustom, calls=%all-reduce-scatter.2 | all-reduce-scatter fusion | flops 90113 | bytes 524800
  270.2 2.5 collective-permute-start.8
  272.7 1.3 collective-permute-done.8
  275.0 42.2 %psum.47 = f32[]{:T(128)} all-reduce(f32[]{:T(128)} %multiply_reduce_fusion), channel_id=1, replica_groups=mesh['space'=16,'chaos'=2] {'space','chaos'}, use_global_device_ids=true, to_apply=%region_14.0 | all-reduce | flops 1 | bytes 8 | tf_op jit(solution)/shard_map/psum | solution.py:83
  318.5 0.8 multiply_subtract_fusion
  (59 shorter events, 9.8 us)
Async XLA Ops:
  2.9 11.0 %collective-permute-start = (f32[84,64]{0,1:T(8,128)S(1)}, f32[84,64]{0,1:T(8,128)S(1)}, u32[]{:S(2)}, u32[]{:S(2)}) collective-permute-start(f32[84,64]{0,1:T(8,128)S(1)} %get-tuple-element.20), channel_id=1, source_target_pairs={{0,2},{2,4},{4,6},{6,8},{8,10},{10,12},{12,14},{14,16},{16,18},{18... | collective-permute-start | bytes 64520 | tf_op jit(solution)/shard_map/ppermute | solution.py:21
  5.3 8.7 %collective-permute-start.1 = (f32[84,64]{0,1:T(8,128)S(1)}, f32[84,64]{0,1:T(8,128)S(1)}, u32[]{:S(2)}, u32[]{:S(2)}) collective-permute-start(f32[84,64]{0,1:T(8,128)S(1)} %get-tuple-element.21), channel_id=1, source_target_pairs={{2,0},{4,2},{6,4},{8,6},{10,8},{12,10},{14,12},{16,14},{18,16},{20... | collective-permute-start | bytes 64520 | tf_op jit(solution)/shard_map/ppermute | solution.py:23
  20.7 14.4 %copy-start.8 = (u32[32]{0:T(128)S(1)}, u32[32]{0:T(128)}, u32[]{:S(2)}) copy-start(u32[32]{0:T(128)} %constant.25) | copy-start | bytes 388
  20.7 15.9 %copy-start = (f32[84,512]{1,0:T(8,128)S(1)}, f32[84,512]{1,0:T(8,128)}, u32[]{:S(2)}) copy-start(f32[84,512]{1,0:T(8,128)} %param.8) | copy-start | bytes 516100
  20.7 15.9 %copy-start.1 = (f32[84,512]{1,0:T(8,128)S(1)}, f32[84,512]{1,0:T(8,128)}, u32[]{:S(2)}) copy-start(f32[84,512]{1,0:T(8,128)} %param.7) | copy-start | bytes 516100
  33.6 2.8 collective-permute-start.6
  84.2 50.2 %copy-start.6 = (f32[84,512]{1,0:T(8,128)}, f32[84,512]{1,0:T(8,128)S(1)}, u32[]{:S(2)}) copy-start(f32[84,512]{1,0:T(8,128)S(1)} %get-tuple-element.13) | copy-start | bytes 516100
  127.2 2.6 collective-permute-start.2
  128.5 5.9 %collective-permute-start.3 = (f32[84,64]{0,1:T(8,128)S(1)}, f32[84,64]{0,1:T(8,128)S(1)}, u32[]{:S(2)}, u32[]{:S(2)}) collective-permute-start(f32[84,64]{0,1:T(8,128)S(1)} %get-tuple-element.19), channel_id=1, source_target_pairs={{2,0},{4,2},{6,4},{8,6},{10,8},{12,10},{14,12},{16,14},{18,16},{20... | collective-permute-start | bytes 64520 | tf_op jit(solution)/shard_map/ppermute | solution.py:23
  141.1 60.1 %copy-start.7 = (f32[84,512]{1,0:T(8,128)S(1)}, f32[84,512]{1,0:T(8,128)}, u32[]{:S(2)}) copy-start(f32[84,512]{1,0:T(8,128)} %copy-done.6) | copy-start | bytes 516100
  152.1 4.7 %collective-permute-start.7 = (f32[4,512]{1,0:T(4,128)S(1)}, f32[4,512]{1,0:T(4,128)S(1)}, u32[]{:S(2)}, u32[]{:S(2)}) collective-permute-start(f32[4,512]{1,0:T(4,128)S(1)} %slice.55), channel_id=1, source_target_pairs={{0,1},{2,3},{4,5},{6,7},{8,9},{10,11},{12,13},{14,15},{16,17},{18,... | collective-permute-start | bytes 24584
  201.9 49.8 %copy-start.4 = (f32[84,512]{1,0:T(8,128)}, f32[84,512]{1,0:T(8,128)S(1)}, u32[]{:S(2)}) copy-start(f32[84,512]{1,0:T(8,128)S(1)} %get-tuple-element.11) | copy-start | bytes 516100
  243.9 7.8 %copy-start.2 = (f32[84,512]{1,0:T(8,128)}, f32[84,512]{1,0:T(8,128)S(1)}, u32[]{:S(2)}) copy-start(f32[84,512]{1,0:T(8,128)S(1)} %multiply_add_fusion.1) | copy-start | bytes 516100
  244.6 2.6 collective-permute-start.4
  245.9 5.8 %collective-permute-start.5 = (f32[84,64]{0,1:T(8,128)S(1)}, f32[84,64]{0,1:T(8,128)S(1)}, u32[]{:S(2)}, u32[]{:S(2)}) collective-permute-start(f32[84,64]{0,1:T(8,128)S(1)} %get-tuple-element.17), channel_id=1, source_target_pairs={{2,0},{4,2},{6,4},{8,6},{10,8},{12,10},{14,12},{16,14},{18,16},{20... | collective-permute-start | bytes 64520 | tf_op jit(solution)/shard_map/ppermute | solution.py:23
  258.5 15.8 %copy-start.3 = (f32[84,512]{1,0:T(8,128)S(1)}, f32[84,512]{1,0:T(8,128)}, u32[]{:S(2)}) copy-start(f32[84,512]{1,0:T(8,128)} %copy-done.2) | copy-start | bytes 516100
  258.5 60.0 %copy-start.5 = (f32[84,512]{1,0:T(8,128)S(1)}, f32[84,512]{1,0:T(8,128)}, u32[]{:S(2)}) copy-start(f32[84,512]{1,0:T(8,128)} %copy-done.4) | copy-start | bytes 516100
  270.2 3.9 %collective-permute-start.8 = (f32[4,512]{1,0:T(4,128)S(1)}, f32[4,512]{1,0:T(4,128)S(1)}, u32[]{:S(2)}, u32[]{:S(2)}) collective-permute-start(f32[4,512]{1,0:T(4,128)S(1)} %slice.56), channel_id=1, source_target_pairs={{0,1},{2,3},{4,5},{6,7},{8,9},{10,11},{12,13},{14,15},{16,17},{18,... | collective-permute-start | bytes 24584
where the time goes:
time: 321 us; the launch traced here: 319 us
  blocking collectives  239 us (74%)
  matrix products  31.2 us (10%)
  starting transfers between devices  16.1 us (5%)
  waiting for transfers between devices  11.9 us (4%)
  between operations  8.45 us (3%)
  local copies, waits for them, and re-layouts  7.34 us (2%)
  other arithmetic  5.86 us (2%)
    psum x3, blocking collectives, squares(): return lax.psum(jnp.sum(residual * residual), ('space', 'chaos'))  126 us
    psum x2, blocking collectives, per_device(): lax.psum(jnp.sum(direction * applied), ('space', 'chaos'))  84.5 us
    unnamed x3, blocking collectives  27.6 us
    dot_general x3, matrix products, spatial_terms(): jnp.einsum('mbk,tbck->tmbc', picked, stiffness, precision=lax.Precision.H...  17.7 us
    ppermute x3, waiting for transfers between devices, with_halo(): lax.ppermute(head, axis, [((i + 1) % count, i) for i in range(ends)])  9.06 us
    dot_general x3, matrix products, apply_operator(): jnp.einsum('tij,tjr->ir', local_cols, spatial, precision=lax.Precision.HI...  7.85 us
    unnamed x3, starting transfers between devices  7.28 us
  transfers between devices with their start and end apart: 9, of which 5 were waited for; matrix products, arithmetic and copies ran while one was open for 2% of the time, Pallas kernels for 0%

commit v1 on v0

v1 whole, which is shorter than its diff:
```python
import functools

import jax
import jax.numpy as jnp
from jax import lax
from jax.experimental import pallas as pl
from jax.experimental.pallas import tpu as pltpu
from jax.sharding import PartitionSpec as P

MESH = pl.DeviceIdType.MESH
ITERS = 3
LANES = 128
SHIFT = 2.75
GAMMA = (0.0, 0.52083333, 0.41666667)
PAIRS = ((0, 0), (0, 1), (1, 1), (0, 2), (1, 2), (2, 2), (0, 3), (1, 3), (2, 3))


def split(x):
    hi = x.astype(jnp.bfloat16)
    lo = (x - hi.astype(jnp.float32)).astype(jnp.bfloat16)
    return hi, lo


def dot_nt(a, b):
    return lax.dot_general(a, b, (((1,), (1,)), ((), ())), preferred_element_type=jnp.float32)


def dot_nn(a, b):
    return lax.dot_general(a, b, (((1,), (0,)), ((), ())), preferred_element_type=jnp.float32)


def low_half(shape):
    return lax.broadcasted_iota(jnp.int32, shape, len(shape) - 1) < LANES // 2


def swap(x):
    return pltpu.roll(x, LANES // 2, 1)


def packed_rows(rows):
    return (rows // 8 + 1) // 2 * 8


def pack(x):
    rows = x.shape[0]
    part = packed_rows(rows)
    return jnp.where(low_half((part, LANES)), x[:part], x[rows - part :])


def unpack(x, rows):
    part = x.shape[0]
    turned = swap(x)
    low = low_half(x.shape)
    top = jnp.where(low, x, turned)
    bottom = jnp.where(low, turned, x)
    return jnp.concatenate([top, bottom[2 * part - rows :]], 0)


def one_way(x):
    return jnp.where(x, 1, 0)


def kernel(
    n_space, n_chaos, stage,
    b_ref, d_ref, k_hbm, col_ref, if_ref, tri_ref, val_ref,
    x_out, r_out,
    kf, khi, klo, c2, cdiag, gb, gd, nat, ef, vec, dg, rodd, reven,
    own_send, halo0, halo_out, halo_in, stat, red1, red2, natv,
    k_sem, gb_send, gb_recv, gd_send, gd_recv, h0_send, h0_recv, h_send, h_recv,
    r1_send, r1_recv, r2_send, r2_recv,
):
    f32 = jnp.float32
    modes, width = b_ref.shape
    hp = gb.shape[1]
    mp = n_chaos * hp
    terms, nbr, block, _ = kf.shape
    nnz = col_ref.shape[0]
    pairs = nbr // 2
    even_terms = (terms - 1) // 2
    s = lax.axis_index("space")
    c = lax.axis_index("chaos")

    k_copy = pltpu.make_async_copy(k_hbm, kf, k_sem)
    k_copy.start()

    barrier = pltpu.get_barrier_semaphore()
    group, place = s // stage, s % stage
    n_group = n_space // stage
    has_left, has_right = s > 0, s < n_space - 1

    def greet(space, chaos):
        pl.semaphore_signal(barrier, inc=1, device_id=(space, chaos), device_id_type=MESH)

    for d in range(1, n_chaos):
        greet(s, (c + d) % n_chaos)
    for d in range(n_chaos):
        @pl.when(has_left)
        def _():
            greet(s - 1, (c + d) % n_chaos)

        @pl.when(has_right)
        def _():
            greet(s + 1, (c + d) % n_chaos)
    for d in range(1, stage):
        greet(group * stage + (place + d) % stage, c)
    for d in range(1, n_group):
        greet(((group + d) % n_group) * stage + place, c)

    own_b = jnp.concatenate([b_ref[...], jnp.zeros((hp - modes, width), f32)], 0) if hp > modes else b_ref[...]
    own_d = jnp.concatenate([d_ref[...], jnp.zeros((hp - modes, width), f32)], 0) if hp > modes else d_ref[...]
    gb[c] = own_b
    gd[c] = own_d
    low_hp = low_half((hp, LANES))
    for q in range(pairs):
        chunk = own_b[:, q * LANES : (q + 1) * LANES]
        turned = swap(chunk)
        natv[0, 2 * q] = jnp.where(low_hp, chunk, turned)
        natv[0, 2 * q + 1] = jnp.where(low_hp, turned, chunk)
    if0, if1 = if_ref[0, 0], if_ref[0, 1]
    own_send[1] = pack(natv[0, if0])
    own_send[0] = pack(natv[0, if1])

    pl.semaphore_wait(
        barrier,
        (n_chaos - 1) + n_chaos * (one_way(has_left) + one_way(has_right)) + (stage - 1) + (n_group - 1),
    )

    def halo0_copy(side, d):
        return pltpu.make_async_remote_copy(
            src_ref=own_send.at[side], dst_ref=halo0.at[side, c],
            send_sem=h0_send.at[side, d], recv_sem=h0_recv.at[side, d],
            device_id=(s + 1 if side == 0 else s - 1, (c + d) % n_chaos), device_id_type=MESH,
        )

    def gather_copy(buf, send, recv, d):
        return pltpu.make_async_remote_copy(
            src_ref=buf.at[c], dst_ref=buf.at[c], send_sem=send.at[d], recv_sem=recv.at[d],
            device_id=(s, (c + d) % n_chaos), device_id_type=MESH,
        )

    for d in range(n_chaos):
        @pl.when(has_right)
        def _():
            halo0_copy(0, d).start()

        @pl.when(has_left)
        def _():
            halo0_copy(1, d).start()
    for d in range(1, n_chaos):
        gather_copy(gb, gb_send, gb_recv, d).start()
    for d in range(1, n_chaos):
        gather_copy(gd, gd_send, gd_recv, d).start()

    second = jnp.where(if1 == if0, jnp.where(if0 == 0, 1, 0), if1)
    small, large = jnp.minimum(if0, second), jnp.maximum(if0, second)

    def block_at(k):
        if isinstance(k, int) and k < 2:
            return if0 if k == 0 else second
        row = k - 2
        row = row + one_way(row >= small)
        return row + one_way(row >= large)

    def place_of(row):
        rest = 2 + row - one_way(if0 < row) - one_way(second < row)
        found = jnp.where(row == if0, 0, jnp.where(row == second, 1, rest))
        return jnp.where(row >= nbr, row, found)

    def slot(mode):
        shift = jnp.zeros_like(mode)
        for h in range(1, n_chaos):
            shift = shift + one_way(mode >= h * modes)
        return mode + (hp - modes) * shift

    entries = tri_ref.shape[1]
    term = tri_ref[0:1, :]
    row = slot(tri_ref[1:2, :])
    col = slot(tri_ref[2:3, :])
    values = val_ref[...]
    hit = lax.broadcasted_iota(jnp.int32, (mp, entries), 0) == row
    spread = jnp.where(hit, values, 0.0)
    cdiag[...] = jnp.broadcast_to(
        jnp.sum(jnp.where(term == 0, spread, 0.0), axis=1, keepdims=True), (mp, LANES)
    )
    spread_hi, spread_lo = split(spread)
    spread2 = jnp.concatenate([spread_hi, spread_lo], 0)
    rows_iota = lax.broadcasted_iota(jnp.int32, (even_terms * mp, entries), 0)
    for parity in range(2):
        first = 1 if parity == 0 else 2
        mine = (term > 0) & (term % 2 == first % 2)
        key = jnp.where(mine, ((term - first) // 2) * mp + col, -1)
        hot = jnp.where(rows_iota == key, 1.0, 0.0).astype(jnp.bfloat16)
        c2[parity] = dot_nt(spread2, hot).astype(jnp.bfloat16)

    k_copy.wait()

    def prepare(j, _):
        for odd in range(2):
            k = 2 * j + odd
            source = jnp.where(k == 0, if0, jnp.where(k == 1, second, block_at(k)))
            for t in range(terms):
                hi, lo = split(kf[t, source])
                if t == 0:
                    at = [even_terms * LANES, even_terms * LANES + block]
                else:
                    tau, late = (t - 1) // 2, (t - 1) % 2
                    at = [tau * LANES + (late ^ odd) * block]
                for a in at:
                    khi[k, a : a + block, :] = hi
                    klo[k, a : a + block, :] = lo
        return 0

    lax.fori_loop(0, pairs, prepare, 0)

    low = low_half((mp, LANES))

    def spread_blocks(buf):
        for q in range(pairs):
            for h in range(n_chaos):
                chunk = buf[h, :, q * LANES : (q + 1) * LANES]
                turned = swap(chunk)
                nat[2 * q, h * hp : (h + 1) * hp] = jnp.where(low_hp, chunk, turned)
                nat[2 * q + 1, h * hp : (h + 1) * hp] = jnp.where(low_hp, turned, chunk)

    for d in range(1, n_chaos):
        gather_copy(gb, gb_send, gb_recv, d).wait()
    spread_blocks(gb)
    for p in range(pairs):
        one, two = nat[block_at(2 * p)], nat[block_at(2 * p + 1)]
        ef[0, 2 * p] = one
        ef[0, 2 * p + 1] = two
        vec[0, p] = jnp.where(low, one, two)

    def fill(side, now, read):
        present = has_left if side == 0 else has_right

        @pl.when(present)
        def _():
            read()

        @pl.when(jnp.logical_not(present))
        def _():
            ef[now, nbr + side] = jnp.zeros((mp, LANES), f32)

    for side in range(2):
        def read_first():
            for d in range(n_chaos):
                halo0_copy(side, d).wait_recv()
            for h in range(n_chaos):
                ef[0, nbr + side, h * hp : (h + 1) * hp] = unpack(halo0[side, h], hp)

        fill(side, 0, read_first)
    for side in range(2):
        @pl.when(has_right if side == 0 else has_left)
        def _():
            for d in range(n_chaos):
                halo0_copy(side, d).wait_send()

    def halo_copy(it, side):
        return pltpu.make_async_remote_copy(
            src_ref=halo_out.at[it, side], dst_ref=halo_in.at[it, side],
            send_sem=h_send.at[it, side], recv_sem=h_recv.at[it, side],
            device_id=(s + 1 if side == 0 else s - 1, c), device_id_type=MESH,
        )

    places = [[place_of(col_ref[n, block_at(k)]) for n in range(nnz)] for k in range(nbr)]
    right_place = place_of(if1)
    sums = {}

    def add_product(i, j, one, two):
        part = jnp.sum((one * two).reshape(mp // 8, 8, LANES), axis=0)
        sums[(i, j)] = sums[(i, j)] + part if (i, j) in sums else part

    for p in range(pairs):
        add_product(0, 0, vec[0, p], vec[0, p])

    scale0 = cdiag[...]
    half_pairs = pairs // 2
    n_odd = even_terms * LANES
    for it in range(ITERS):
        now, later = it % 2, (it + 1) % 2
        for half in range(2):
            zeros = []
            for step in range(half_pairs):
                p = half * half_pairs + step
                made = []
                for odd in range(2):
                    k = 2 * p + odd
                    at = places[k]
                    picked = jnp.concatenate(
                        [
                            jnp.where(low, ef[now, at[2 * m]], ef[now, at[2 * m + 1]])
                            for m in range(nnz // 2)
                        ],
                        1,
                    )
                    hi, lo = split(picked)
                    both = dot_nt(jnp.concatenate([hi, lo], 0), khi[k])
                    made.append(both[:mp] + both[mp:] + dot_nt(hi, klo[k]))
                first, next_ = made
                to = pl.ds(step * LANES, LANES)
                for tau in range(even_terms):
                    a = first[:, tau * LANES : (tau + 1) * LANES]
                    b = next_[:, tau * LANES : (tau + 1) * LANES]
                    hi, lo = split(jnp.where(low, a, b))
                    rodd[0, tau * mp : (tau + 1) * mp, to] = hi
                    rodd[1, tau * mp : (tau + 1) * mp, to] = lo
                    hi, lo = split(jnp.where(low, b, a))
                    reven[0, tau * mp : (tau + 1) * mp, to] = hi
                    reven[1, tau * mp : (tau + 1) * mp, to] = lo
                zeros.append(jnp.where(low, first[:, n_odd:], next_[:, n_odd:]))
            coupled = []
            for parity, rhs in ((0, rodd), (1, reven)):
                both = dot_nn(c2[parity], rhs[0])
                coupled.append(both[:mp] + both[mp:] + dot_nn(c2[parity, :mp], rhs[1]))
            if it == 0 and half == 0:
                for d in range(1, n_chaos):
                    gather_copy(gd, gd_send, gd_recv, d).wait()
                spread_blocks(gd)
                for p in range(pairs):
                    one, two = nat[block_at(2 * p)], nat[block_at(2 * p + 1)]
                    dg[p] = jnp.where(low, one, two) - SHIFT
            for step in range(half_pairs):
                p = half * half_pairs + step
                at = slice(step * LANES, (step + 1) * LANES)
                new = coupled[0][:, at] + swap(coupled[1][:, at]) + scale0 * zeros[step]
                new = dg[p] * vec[it, p] + new
                if it > 0:
                    new = new - GAMMA[it] * vec[it - 1, p]
                vec[it + 1, p] = new
                for j in range(it + 1):
                    add_product(j, it + 1, vec[j, p], new)
                if it < ITERS - 1:
                    add_product(it + 1, it + 1, new, new)
                    turned = swap(new)
                    ef[later, 2 * p] = jnp.where(low, new, turned)
                    ef[later, 2 * p + 1] = jnp.where(low, turned, new)
            if it < ITERS - 1 and half == 0:
                halo_out[it, 1] = pack(ef[later, 0])
                halo_out[it, 0] = pack(ef[later, right_place])

                @pl.when(has_right)
                def _():
                    halo_copy(it, 0).start()

                @pl.when(has_left)
                def _():
                    halo_copy(it, 1).start()
        if it < ITERS - 1:
            for side in range(2):
                def read_next():
                    halo_copy(it, side).wait_recv()
                    ef[later, nbr + side] = unpack(halo_in[it, side], mp)

                fill(side, later, read_next)
            for side in range(2):
                @pl.when(has_right if side == 0 else has_left)
                def _():
                    halo_copy(it, side).wait_send()

    stat[...] = jnp.zeros_like(stat)
    for e, pair in enumerate(PAIRS):
        stat[e : e + 1, :] = jnp.sum(sums[pair], axis=0, keepdims=True)

    def reduce_copy(level, d):
        if level == 0:
            target, src, dst, send, recv = group * stage + (place + d) % stage, stat, red1.at[place], r1_send, r1_recv
        else:
            target, src, dst, send, recv = ((group + d) % n_group) * stage + place, stat, red2.at[group], r2_send, r2_recv
        return pltpu.make_async_remote_copy(
            src_ref=src, dst_ref=dst, send_sem=send.at[d], recv_sem=recv.at[d],
            device_id=(target, c), device_id_type=MESH,
        )

    red1[place] = stat[...]
    for d in range(1, stage):
        reduce_copy(0, d).start()

    mine = pl.ds(pl.multiple_of(c * hp, 8), hp)
    back = [place_of(jnp.int32(k)) for k in range(nbr)]
    for j in range(ITERS + 1):
        for p in range(pairs):
            chunk = vec[j, p, mine, :]
            turned = swap(chunk)
            natv[j, 2 * p] = jnp.where(low_hp, chunk, turned)
            natv[j, 2 * p + 1] = jnp.where(low_hp, turned, chunk)

    for d in range(1, stage):
        reduce_copy(0, d).wait()
    total = red1[0]
    for g in range(1, stage):
        total = total + red1[g]
    stat[...] = total
    red2[group] = total
    for d in range(1, n_group):
        reduce_copy(1, d).start()
    for d in range(1, n_group):
        reduce_copy(1, d).wait()
    total = red2[0]
    for g in range(1, n_group):
        total = total + red2[g]
    total = jnp.sum(total, axis=1, keepdims=True)
    gram = {}
    for e, (i, j) in enumerate(PAIRS):
        gram[(i, j)] = gram[(j, i)] = total[e : e + 1, :]

    def inner(one, two):
        value = None
        for i, a in one.items():
            for j, b in two.items():
                part = a * b * gram[(i, j)]
                value = part if value is None else value + part
        return value

    def plus(one, scale, two):
        result = dict(one)
        for i, a in two.items():
            result[i] = result[i] + scale * a if i in result else scale * a
        return result

    def image_of(vector):
        result = {}
        for k, a in vector.items():
            result = plus(result, a, {k: jnp.full((1, 1), SHIFT, f32), k + 1: jnp.ones((1, 1), f32)})
            if k > 0:
                result = plus(result, a, {k - 1: jnp.full((1, 1), GAMMA[k], f32)})
        return result

    residual = {0: jnp.ones((1, 1), f32)}
    direction = dict(residual)
    field = {}
    norm_now = gram[(0, 0)]
    for it in range(ITERS):
        image = image_of(direction)
        alpha = norm_now / inner(direction, image)
        field = plus(field, alpha, direction)
        residual = plus(residual, -alpha, image)
        if it < ITERS - 1:
            norm_next = inner(residual, residual)
            direction = plus(residual, norm_next / norm_now, direction)
            norm_now = norm_next

    for q in range(pairs):
        parts = []
        for j in range(ITERS + 1):
            parts.append(jnp.where(low_hp, natv[j, back[2 * q]], natv[j, back[2 * q + 1]]))
        for coefs, out in ((field, x_out), (residual, r_out)):
            value = None
            for j, a in coefs.items():
                part = a * parts[j]
                value = part if value is None else value + part
            out[:, q * LANES : (q + 1) * LANES] = value[:modes]


def per_device(right_side, diagonal, stiffness, columns, interface, triples, coupling_values):
    n_space, n_chaos = lax.axis_size("space"), lax.axis_size("chaos")
    modes, width = right_side.shape
    terms, nbr, block, depth = stiffness.shape
    hp = (modes + 7) // 8 * 8
    mp = n_chaos * hp
    pairs = nbr // 2
    even_terms = (terms - 1) // 2
    cols = even_terms * LANES + 2 * block
    stage = 1
    while stage * stage < n_space:
        stage *= 2
    n_group = n_space // stage
    f32, bf16 = jnp.float32, jnp.bfloat16
    vmem = pl.BlockSpec(memory_space=pltpu.VMEM)
    smem = pl.BlockSpec(memory_space=pltpu.SMEM)
    dma = pltpu.SemaphoreType.DMA
    out = jax.ShapeDtypeStruct((modes, width), f32)
    return pl.pallas_call(
        functools.partial(kernel, n_space, n_chaos, stage),
        out_shape=(out, out),
        in_specs=[vmem, vmem, pl.BlockSpec(memory_space=pl.ANY), smem, smem, vmem, vmem],
        out_specs=(vmem, vmem),
        scratch_shapes=[
            pltpu.VMEM(stiffness.shape, f32),
            pltpu.VMEM((nbr, cols, depth), bf16),
            pltpu.VMEM((nbr, cols, depth), bf16),
            pltpu.VMEM((2, 2 * mp, even_terms * mp), bf16),
            pltpu.VMEM((mp, LANES), f32),
            pltpu.VMEM((n_chaos, hp, width), f32),
            pltpu.VMEM((n_chaos, hp, width), f32),
            pltpu.VMEM((nbr, mp, LANES), f32),
            pltpu.VMEM((2, nbr + 2, mp, LANES), f32),
            pltpu.VMEM((ITERS + 1, pairs, mp, LANES), f32),
            pltpu.VMEM((pairs, mp, LANES), f32),
            pltpu.VMEM((2, even_terms * mp, pairs // 2 * LANES), bf16),
            pltpu.VMEM((2, even_terms * mp, pairs // 2 * LANES), bf16),
            pltpu.VMEM((2, packed_rows(hp), LANES), f32),
            pltpu.VMEM((2, n_chaos, packed_rows(hp), LANES), f32),
            pltpu.VMEM((ITERS - 1, 2, packed_rows(mp), LANES), f32),
            pltpu.VMEM((ITERS - 1, 2, packed_rows(mp), LANES), f32),
            pltpu.VMEM((16, LANES), f32),
            pltpu.VMEM((stage, 16, LANES), f32),
            pltpu.VMEM((n_group, 16, LANES), f32),
            pltpu.VMEM((ITERS + 1, nbr, hp, LANES), f32),
            dma,
            dma((n_chaos,)), dma((n_chaos,)), dma((n_chaos,)), dma((n_chaos,)),
            dma((2, n_chaos)), dma((2, n_chaos)),
            dma((ITERS - 1, 2)), dma((ITERS - 1, 2)),
            dma((stage,)), dma((stage,)), dma((n_group,)), dma((n_group,)),
        ],
        compiler_params=pltpu.CompilerParams(
            collective_id=0, has_side_effects=True, vmem_limit_bytes=56 * 1024 * 1024
        ),
        name="solve",
    )(
        right_side, diagonal, stiffness, columns.T, interface, triples.T,
        coupling_values.reshape(1, -1),
    )


def solution(mesh):
    placed = (
        P("chaos", "space"),
        P("chaos", "space"),
        P(None, "space", None, None),
        P("space", None),
        P("space", None),
        P(),
        P(),
    )
    return jax.shard_map(
        per_device,
        mesh=mesh,
        in_specs=placed,
        out_specs=(P("chaos", "space"), P("chaos", "space")),
        check_vma=False,
    )
```

time: 321 us -> 41.7 us (0.13)
  blocking collectives: 239 us -> 0 us
  Pallas kernels: 0 us -> 36.3 us
  matrix products: 31.2 us -> 0 us
  starting transfers between devices: 16.1 us -> 0 us
  waiting for transfers between devices: 11.9 us -> 0 us
  between operations: 8.45 us -> 0.64 us
  other arithmetic: 5.86 us -> 0 us
    psum x5 -> x0, blocking collectives: 211 us -> none  [the longest x3 126 us: squares(): return lax.psum(jnp.sum(residual * residual), ('space', 'chaos'))]
    pallas_call x0 -> x1, Pallas kernels: none -> 36.3 us  [per_device(): pl.pallas_call(functools.partial(kernel, n_space, n_chaos, stage), out_sh...]
    dot_general x7 -> x0, matrix products: 31.2 us -> none  [the longest x3 17.7 us: spatial_terms(): jnp.einsum('mbk,tbck->tmbc', picked, stiffness, precision=lax.Precision.H...]
    unnamed x3 -> x0, blocking collectives: 27.6 us -> none
    ppermute x6 -> x0, waiting for transfers between devices: 9.07 us -> none  [the longest x3 9.06 us: with_halo(): lax.ppermute(head, axis, [((i + 1) % count, i) for i in range(ends)])]
    ppermute x6 -> x0, starting transfers between devices: 8.82 us -> none  [the longest x3 4.94 us: with_halo(): lax.ppermute(tail, axis, [(i, (i + 1) % count) for i in range(ends)])]
    unnamed x3 -> x0, starting transfers between devices: 7.28 us -> none
    gather x6 -> x0, local copies, waits for them, and re-layouts: 3.52 us -> none  [the longest x3 1.85 us: spatial_terms(): extended[:, columns.reshape(-1), :]]
  transfers between devices with their start and end apart: 9 -> 0, of which waited for: 5 -> 0; matrix products, arithmetic and copies ran while one was open for 2% -> 0% of each run, Pallas kernels for 0% -> 0%
where the time goes in v1:
time: 41.7 us; the launch traced here: 41.5 us
  Pallas kernels  36.3 us (87%)
  local copies, waits for them, and re-layouts  4.48 us (11%)
  between operations  0.64 us (2%)
    pallas_call x1, Pallas kernels, per_device(): pl.pallas_call(functools.partial(kernel, n_space, n_chaos, stage), out_sh...  36.3 us
    unnamed x2, local copies, waits for them, and re-layouts  3.21 us
    reshape x1, local copies, waits for them, and re-layouts, per_device(): coupling_values.reshape(1, -1)  1.27 us

profile of v1, /device:TPU:0, one launch (start us, length us, event | category | flops | bytes accessed | tf_op | source)
XLA Modules:
  0.0 41.5 jit_solution(16618719638454047727)
XLA Ops:
  0.6 1.3 %reshape.7.val_ref = f32[1,885]{1,0:T(1,128)} reshape(f32[885]{0:T(1024)} %param.13) | data formatting | bytes 7080 | tf_op jit(solution)/shard_map/reshape | solution.py:512
  1.9 36.3 %solve.1 = (f32[84,512]{1,0:T(8,128)}, f32[84,512]{1,0:T(8,128)}) custom-call(f32[84,512]{1,0:T(8,128)} %b_ref.1, f32[84,512]{1,0:T(8,128)} %d_ref.1, f32[9,8,64,256]{3,2,1,0:T(8,128)} %k_hbm.1, s32[4,8]{1,0:T(4,128)} %bitcast.3, s32[1,2]{1,0:T(1,128)} %if_ref.1, s32[3,885]{1,0:T(4,128)} %bitcast.2, f32[1,885]{1,0:T(1,128)} %reshape.7.val_ref), custom_call_target="tpu_custom_call" | custom-call | tf_op jit(solution)/shard_map/solve/pallas_call | solution.py:473
  38.3 1.6 %copy.11 = f32[84,512]{1,0:T(8,128)} copy(f32[84,512]{1,0:T(8,128)} %get-tuple-element.4) | data formatting | bytes 344064
  39.9 1.6 %copy.12 = f32[84,512]{1,0:T(8,128)} copy(f32[84,512]{1,0:T(8,128)} %get-tuple-element.5) | data formatting | bytes 344064

commit v2 on v1

--- a/solution.py
+++ b/solution.py
@@ -63,9 +63,9 @@
 def kernel(
     n_space, n_chaos, stage,
     b_ref, d_ref, k_hbm, col_ref, if_ref, tri_ref, val_ref,
-    x_out, r_out,
-    kf, khi, klo, c2, cdiag, gb, gd, nat, ef, vec, dg, rodd, reven,
-    own_send, halo0, halo_out, halo_in, stat, red1, red2, natv,
+    v0_out, v1_out, v2_out, v3_out, coef_out,
+    kf, khi, klo, c3, cdiag, gb, gd, nat, ef0, ef1, vec, dg, picked, rodd, reven,
+    own_send, own_blocks, halo0, halo_out, halo_in, stat, red1, red2, natv,
     k_sem, gb_send, gb_recv, gd_send, gd_recv, h0_send, h0_recv, h_send, h_recv,
     r1_send, r1_recv, r2_send, r2_recv,
 ):
@@ -77,6 +77,8 @@
     nnz = col_ref.shape[0]
     pairs = nbr // 2
     even_terms = (terms - 1) // 2
+    depth = rodd.shape[2]
+    ef = (ef0, ef1)
     s = lax.axis_index("space")
     c = lax.axis_index("chaos")
 
@@ -114,11 +116,11 @@
     for q in range(pairs):
         chunk = own_b[:, q * LANES : (q + 1) * LANES]
         turned = swap(chunk)
-        natv[0, 2 * q] = jnp.where(low_hp, chunk, turned)
-        natv[0, 2 * q + 1] = jnp.where(low_hp, turned, chunk)
+        own_blocks[2 * q] = jnp.where(low_hp, chunk, turned)
+        own_blocks[2 * q + 1] = jnp.where(low_hp, turned, chunk)
     if0, if1 = if_ref[0, 0], if_ref[0, 1]
-    own_send[1] = pack(natv[0, if0])
-    own_send[0] = pack(natv[0, if1])
+    own_send[1] = pack(own_blocks[if0])
+    own_send[0] = pack(own_blocks[if1])
 
     pl.semaphore_wait(
         barrier,
@@ -176,7 +178,7 @@
     term = tri_ref[0:1, :]
     row = slot(tri_ref[1:2, :])
     col = slot(tri_ref[2:3, :])
-    values = val_ref[...]
+    values = val_ref[...].reshape(1, entries)
     hit = lax.broadcasted_iota(jnp.int32, (mp, entries), 0) == row
     spread = jnp.where(hit, values, 0.0)
     cdiag[...] = jnp.broadcast_to(
@@ -184,13 +186,22 @@
     )
     spread_hi, spread_lo = split(spread)
     spread2 = jnp.concatenate([spread_hi, spread_lo], 0)
-    rows_iota = lax.broadcasted_iota(jnp.int32, (even_terms * mp, entries), 0)
+    rows_iota = lax.broadcasted_iota(jnp.int32, (depth, entries), 0)
     for parity in range(2):
         first = 1 if parity == 0 else 2
         mine = (term > 0) & (term % 2 == first % 2)
         key = jnp.where(mine, ((term - first) // 2) * mp + col, -1)
         hot = jnp.where(rows_iota == key, 1.0, 0.0).astype(jnp.bfloat16)
-        c2[parity] = dot_nt(spread2, hot).astype(jnp.bfloat16)
+        both = dot_nt(spread2, hot).astype(jnp.bfloat16)
+        c3[parity, :, :depth] = both[:mp]
+        c3[parity, :, depth : 2 * depth] = both[mp:]
+        c3[parity, :, 2 * depth :] = both[:mp]
+    if depth > even_terms * mp:
+        rest = jnp.zeros((depth - even_terms * mp, rodd.shape[3]), jnp.bfloat16)
+        for half in range(2):
+            for part in range(2):
+                rodd[half, part, even_terms * mp :, :] = rest
+                reven[half, part, even_terms * mp :, :] = rest
 
     k_copy.wait()
 
@@ -227,8 +238,8 @@
     spread_blocks(gb)
     for p in range(pairs):
         one, two = nat[block_at(2 * p)], nat[block_at(2 * p + 1)]
-        ef[0, 2 * p] = one
-        ef[0, 2 * p + 1] = two
+        ef0[2 * p] = one
+        ef0[2 * p + 1] = two
         vec[0, p] = jnp.where(low, one, two)
 
     def fill(side, now, read):
@@ -240,14 +251,14 @@
 
         @pl.when(jnp.logical_not(present))
         def _():
-            ef[now, nbr + side] = jnp.zeros((mp, LANES), f32)
+            ef[now][nbr + side] = jnp.zeros((mp, LANES), f32)
 
     for side in range(2):
         def read_first():
             for d in range(n_chaos):
                 halo0_copy(side, d).wait_recv()
             for h in range(n_chaos):
-                ef[0, nbr + side, h * hp : (h + 1) * hp] = unpack(halo0[side, h], hp)
+                ef0[nbr + side, h * hp : (h + 1) * hp] = unpack(halo0[side, h], hp)
 
         fill(side, 0, read_first)
     for side in range(2):
@@ -277,42 +288,48 @@
     scale0 = cdiag[...]
     half_pairs = pairs // 2
     n_odd = even_terms * LANES
+    wide = nnz * block
     for it in range(ITERS):
         now, later = it % 2, (it + 1) % 2
         for half in range(2):
             zeros = []
             for step in range(half_pairs):
                 p = half * half_pairs + step
-                made = []
-                for odd in range(2):
-                    k = 2 * p + odd
+                for k in (2 * p, 2 * p + 1):
                     at = places[k]
-                    picked = jnp.concatenate(
-                        [
-                            jnp.where(low, ef[now, at[2 * m]], ef[now, at[2 * m + 1]])
-                            for m in range(nnz // 2)
-                        ],
-                        1,
-                    )
-                    hi, lo = split(picked)
-                    both = dot_nt(jnp.concatenate([hi, lo], 0), khi[k])
-                    made.append(both[:mp] + both[mp:] + dot_nt(hi, klo[k]))
-                first, next_ = made
+                    for m in range(nnz // 2):
+                        hi, lo = split(jnp.where(low, ef[now][at[2 * m]], ef[now][at[2 * m + 1]]))
+                        picked[k, :, m * LANES : (m + 1) * LANES] = hi
+                        picked[k, :, wide + m * LANES : wide + (m + 1) * LANES] = lo
+            for step in range(half_pairs):
+                p = half * half_pairs + step
                 to = pl.ds(step * LANES, LANES)
-                for tau in range(even_terms):
-                    a = first[:, tau * LANES : (tau + 1) * LANES]
-                    b = next_[:, tau * LANES : (tau + 1) * LANES]
-                    hi, lo = split(jnp.where(low, a, b))
-                    rodd[0, tau * mp : (tau + 1) * mp, to] = hi
-                    rodd[1, tau * mp : (tau + 1) * mp, to] = lo
-                    hi, lo = split(jnp.where(low, b, a))
-                    reven[0, tau * mp : (tau + 1) * mp, to] = hi
-                    reven[1, tau * mp : (tau + 1) * mp, to] = lo
-                zeros.append(jnp.where(low, first[:, n_odd:], next_[:, n_odd:]))
+                for start in range(0, n_odd + 2 * block, 2 * LANES):
+                    stop = min(start + 2 * LANES, n_odd + 2 * block)
+                    made = []
+                    for k in (2 * p, 2 * p + 1):
+                        hi, lo = picked[k, :, :wide], picked[k, :, wide:]
+                        k_hi, k_lo = khi[k, start:stop, :], klo[k, start:stop, :]
+                        made.append(
+                            dot_nt(jnp.concatenate([hi, lo, hi], 1), jnp.concatenate([k_hi, k_hi, k_lo], 1))
+                        )
+                    for piece in range(start, stop, LANES):
+                        tau = piece // LANES
+                        a = made[0][:, piece - start : piece - start + LANES]
+                        b = made[1][:, piece - start : piece - start + LANES]
+                        if piece == n_odd:
+                            zeros.append(jnp.where(low, a, b))
+                            continue
+                        hi, lo = split(jnp.where(low, a, b))
+                        rodd[half, 0, tau * mp : (tau + 1) * mp, to] = hi
+                        rodd[half, 1, tau * mp : (tau + 1) * mp, to] = lo
+                        hi, lo = split(jnp.where(low, b, a))
+                        reven[half, 0, tau * mp : (tau + 1) * mp, to] = hi
+                        reven[half, 1, tau * mp : (tau + 1) * mp, to] = lo
             coupled = []
             for parity, rhs in ((0, rodd), (1, reven)):
-                both = dot_nn(c2[parity], rhs[0])
-                coupled.append(both[:mp] + both[mp:] + dot_nn(c2[parity, :mp], rhs[1]))
+                hi, lo = rhs[half, 0], rhs[half, 1]
+                coupled.append(dot_nn(c3[parity], jnp.concatenate([hi, hi, lo], 0)))
             if it == 0 and half == 0:
                 for d in range(1, n_chaos):
                     gather_copy(gd, gd_send, gd_recv, d).wait()
@@ -333,11 +350,11 @@
                 if it < ITERS - 1:
                     add_product(it + 1, it + 1, new, new)
                     turned = swap(new)
-                    ef[later, 2 * p] = jnp.where(low, new, turned)
-                    ef[later, 2 * p + 1] = jnp.where(low, turned, new)
+                    ef[later][2 * p] = jnp.where(low, new, turned)
+                    ef[later][2 * p + 1] = jnp.where(low, turned, new)
             if it < ITERS - 1 and half == 0:
-                halo_out[it, 1] = pack(ef[later, 0])
-                halo_out[it, 0] = pack(ef[later, right_place])
+                halo_out[it, 1] = pack(ef[later][0])
+                halo_out[it, 0] = pack(ef[later][right_place])
 
                 @pl.when(has_right)
                 def _():
@@ -350,7 +367,7 @@
             for side in range(2):
                 def read_next():
                     halo_copy(it, side).wait_recv()
-                    ef[later, nbr + side] = unpack(halo_in[it, side], mp)
+                    ef[later][nbr + side] = unpack(halo_in[it, side], mp)
 
                 fill(side, later, read_next)
             for side in range(2):
@@ -384,6 +401,10 @@
             turned = swap(chunk)
             natv[j, 2 * p] = jnp.where(low_hp, chunk, turned)
             natv[j, 2 * p + 1] = jnp.where(low_hp, turned, chunk)
+    for j, out in enumerate((v0_out, v1_out, v2_out, v3_out)):
+        for q in range(pairs):
+            chunk = jnp.where(low_hp, natv[j, back[2 * q]], natv[j, back[2 * q + 1]])
+            out[:, q * LANES : (q + 1) * LANES] = chunk[:modes]
 
     for d in range(1, stage):
         reduce_copy(0, d).wait()
@@ -440,16 +461,9 @@
             direction = plus(residual, norm_next / norm_now, direction)
             norm_now = norm_next
 
-    for q in range(pairs):
-        parts = []
-        for j in range(ITERS + 1):
-            parts.append(jnp.where(low_hp, natv[j, back[2 * q]], natv[j, back[2 * q + 1]]))
-        for coefs, out in ((field, x_out), (residual, r_out)):
-            value = None
-            for j, a in coefs.items():
-                part = a * parts[j]
-                value = part if value is None else value + part
-            out[:, q * LANES : (q + 1) * LANES] = value[:modes]
+    for coefs, first in ((field, 0), (residual, 8)):
+        for j, a in coefs.items():
+            coef_out[first + j : first + j + 1, :] = jnp.broadcast_to(a, (1, LANES))
 
 
 def per_device(right_side, diagonal, stiffness, columns, interface, triples, coupling_values):
@@ -470,26 +484,30 @@
     smem = pl.BlockSpec(memory_space=pltpu.SMEM)
     dma = pltpu.SemaphoreType.DMA
     out = jax.ShapeDtypeStruct((modes, width), f32)
-    return pl.pallas_call(
+    whole_depth = -(-even_terms * mp // 256) * 256
+    *basis, coefs = pl.pallas_call(
         functools.partial(kernel, n_space, n_chaos, stage),
-        out_shape=(out, out),
+        out_shape=(out,) * (ITERS + 1) + (jax.ShapeDtypeStruct((16, LANES), f32),),
         in_specs=[vmem, vmem, pl.BlockSpec(memory_space=pl.ANY), smem, smem, vmem, vmem],
-        out_specs=(vmem, vmem),
+        out_specs=(vmem,) * (ITERS + 2),
         scratch_shapes=[
             pltpu.VMEM(stiffness.shape, f32),
             pltpu.VMEM((nbr, cols, depth), bf16),
             pltpu.VMEM((nbr, cols, depth), bf16),
-            pltpu.VMEM((2, 2 * mp, even_terms * mp), bf16),
+            pltpu.VMEM((2, mp, 3 * whole_depth), bf16),
             pltpu.VMEM((mp, LANES), f32),
             pltpu.VMEM((n_chaos, hp, width), f32),
             pltpu.VMEM((n_chaos, hp, width), f32),
             pltpu.VMEM((nbr, mp, LANES), f32),
-            pltpu.VMEM((2, nbr + 2, mp, LANES), f32),
+            pltpu.VMEM((nbr + 2, mp, LANES), f32),
+            pltpu.VMEM((nbr + 2, mp, LANES), f32),
             pltpu.VMEM((ITERS + 1, pairs, mp, LANES), f32),
             pltpu.VMEM((pairs, mp, LANES), f32),
-            pltpu.VMEM((2, even_terms * mp, pairs // 2 * LANES), bf16),
-            pltpu.VMEM((2, even_terms * mp, pairs // 2 * LANES), bf16),
+            pltpu.VMEM((nbr, mp, 2 * depth), bf16),
+            pltpu.VMEM((2, 2, whole_depth, pairs // 2 * LANES), bf16),
+            pltpu.VMEM((2, 2, whole_depth, pairs // 2 * LANES), bf16),
             pltpu.VMEM((2, packed_rows(hp), LANES), f32),
+            pltpu.VMEM((nbr, hp, LANES), f32),
             pltpu.VMEM((2, n_chaos, packed_rows(hp), LANES), f32),
             pltpu.VMEM((ITERS - 1, 2, packed_rows(mp), LANES), f32),
             pltpu.VMEM((ITERS - 1, 2, packed_rows(mp), LANES), f32),
@@ -504,13 +522,16 @@
             dma((stage,)), dma((stage,)), dma((n_group,)), dma((n_group,)),
         ],
         compiler_params=pltpu.CompilerParams(
-            collective_id=0, has_side_effects=True, vmem_limit_bytes=56 * 1024 * 1024
+            collective_id=0, has_side_effects=True, vmem_limit_bytes=60 * 1024 * 1024
         ),
         name="solve",
     )(
         right_side, diagonal, stiffness, columns.T, interface, triples.T,
-        coupling_values.reshape(1, -1),
+        coupling_values,
     )
+    field = sum(coefs[j, 0] * basis[j] for j in range(ITERS))
+    residual = sum(coefs[8 + j, 0] * basis[j] for j in range(ITERS + 1))
+    return field, residual
 
 
 def solution(mesh):

time: 41.7 us -> 44.9 us (1.077)
  other arithmetic: 0 us -> 6.24 us
  local copies, waits for them, and re-layouts: 4.48 us -> 1.43 us
    add x0 -> x1, other arithmetic: none -> 6.24 us  [per_device(): residual = sum((coefs[8 + j, 0] * basis[j] for j in range(ITERS + 1)))]
    unnamed x2 -> x0, local copies, waits for them, and re-layouts: 3.21 us -> none
    slice x0 -> x1, local copies, waits for them, and re-layouts: none -> 1.43 us  [per_device(): residual = sum((coefs[8 + j, 0] * basis[j] for j in range(ITERS + 1)))]
    reshape x1 -> x0, local copies, waits for them, and re-layouts: 1.27 us -> none  [per_device(): coupling_values.reshape(1, -1)]
where the time goes in v2:
time: 44.9 us; the launch traced here: 44.8 us
  Pallas kernels  36.4 us (81%)
  other arithmetic  6.24 us (14%)
  local copies, waits for them, and re-layouts  1.43 us (3%)
  between operations  0.64 us (1%)
    pallas_call x1, Pallas kernels, per_device(): pl.pallas_call(functools.partial(kernel, n_space, n_chaos, stage), out_sh...  36.4 us
    add x1, other arithmetic, per_device(): residual = sum((coefs[8 + j, 0] * basis[j] for j in range(ITERS + 1)))  6.24 us
    slice x1, local copies, waits for them, and re-layouts, per_device(): residual = sum((coefs[8 + j, 0] * basis[j] for j in range(ITERS + 1)))  1.43 us

profile of v2, /device:TPU:0, one launch (start us, length us, event | category | flops | bytes accessed | tf_op | source)
XLA Modules:
  0.0 44.8 jit_solution(6840701538857837882)
XLA Ops:
  0.6 36.4 %solve.1 = (f32[84,512]{1,0:T(8,128)}, f32[84,512]{1,0:T(8,128)}, f32[84,512]{1,0:T(8,128)}, f32[84,512]{1,0:T(8,128)}, f32[16,128]{1,0:T(8,128)}) custom-call(f32[84,512]{1,0:T(8,128)} %b_ref.1, f32[84,512]{1,0:T(8,128)} %d_ref.1, f32[9,8,64,256]{3,2,1,0:T(8,128)} %k_hbm.1, s32[4,8]{1,0:T(4,128)} %bitcast.10, s32[1,2]{1,0:T(1,128)} %if_ref.1, ...), custom_call_target="tpu_custom_call" | custom-call | tf_op jit(solution)/shard_map/solve/pallas_call | solution.py:488
  37.1 1.4 %fusion = (f32[1,1]{1,0:T(1,128)}, f32[1,1]{1,0:T(1,128)}, f32[1,1]{1,0:T(1,128)}, f32[1,1]{1,0:T(1,128)}, f32[1,1]{1,0:T(1,128)}, /*index=5*/f32[1,1]{1,0:T(1,128)}, f32[1,1]{1,0:T(1,128)}) fusion(f32[16,128]{1,0:T(8,128)} %get-tuple-element.7), kind=kLoop, calls=%fused_computation.2 | loop fusion | bytes 56 | tf_op jit(solution)/shard_map/slice | solution.py:533
  38.5 6.2 %multiply_add_fusion = (f32[84,512]{1,0:T(8,128)}, f32[84,512]{1,0:T(8,128)}) fusion(f32[84,512]{1,0:T(8,128)} %get-tuple-element.11, f32[84,512]{1,0:T(8,128)} %get-tuple-element.10, f32[84,512]{1,0:T(8,128)} %get-tuple-element.9, f32[84,512]{1,0:T(8,128)} %get-tuple-element.8, f32[]{:T(128)} %bitcast.8, f32[]{:T(128)} %bitcast.7, f32[]{:T(128)} %bitcast.6, ...), kind=kLoop, calls=%fused_computation | loop fusion | flops 516096 | bytes 1032220 | tf_op jit(solution)/shard_map/add | solution.py:533

commit v3 on v2

--- a/solution.py
+++ b/solution.py
@@ -19,10 +19,6 @@
     hi = x.astype(jnp.bfloat16)
     lo = (x - hi.astype(jnp.float32)).astype(jnp.bfloat16)
     return hi, lo
-
-
-def dot_nt(a, b):
-    return lax.dot_general(a, b, (((1,), (1,)), ((), ())), preferred_element_type=jnp.float32)
 
 
 def dot_nn(a, b):
@@ -186,13 +182,20 @@
     )
     spread_hi, spread_lo = split(spread)
     spread2 = jnp.concatenate([spread_hi, spread_lo], 0)
-    rows_iota = lax.broadcasted_iota(jnp.int32, (depth, entries), 0)
+    padded = -(-entries // LANES) * LANES
+    spread2 = jnp.concatenate([spread2, jnp.zeros((2 * mp, padded - entries), spread2.dtype)], 1)
+    lanes_iota = lax.broadcasted_iota(jnp.int32, (LANES, depth), 1)
     for parity in range(2):
         first = 1 if parity == 0 else 2
-        mine = (term > 0) & (term % 2 == first % 2)
-        key = jnp.where(mine, ((term - first) // 2) * mp + col, -1)
-        hot = jnp.where(rows_iota == key, 1.0, 0.0).astype(jnp.bfloat16)
-        both = dot_nt(spread2, hot).astype(jnp.bfloat16)
+        mine = (term > 0) & ((term & 1) == (first & 1))
+        key = jnp.where(mine, ((term - first) >> 1) * mp + col, -1)
+        key = jnp.concatenate([key, jnp.full((1, padded - entries), -1, jnp.int32)], 1)
+        hot = []
+        for n in range(0, padded, LANES):
+            down = jnp.broadcast_to(key[:, n : n + LANES], (LANES, LANES)).T
+            down = jnp.concatenate([down] * (depth // LANES), 1)
+            hot.append(jnp.where(lanes_iota == down, 1.0, 0.0).astype(jnp.bfloat16))
+        both = dot_nn(spread2, jnp.concatenate(hot, 0)).astype(jnp.bfloat16)
         c3[parity, :, :depth] = both[:mp]
         c3[parity, :, depth : 2 * depth] = both[mp:]
         c3[parity, :, 2 * depth :] = both[:mp]
@@ -209,16 +212,14 @@
         for odd in range(2):
             k = 2 * j + odd
             source = jnp.where(k == 0, if0, jnp.where(k == 1, second, block_at(k)))
-            for t in range(terms):
-                hi, lo = split(kf[t, source])
-                if t == 0:
-                    at = [even_terms * LANES, even_terms * LANES + block]
+            for tau in range(even_terms + 1):
+                if tau == even_terms:
+                    one = two = kf[0, source]
                 else:
-                    tau, late = (t - 1) // 2, (t - 1) % 2
-                    at = [tau * LANES + (late ^ odd) * block]
-                for a in at:
-                    khi[k, a : a + block, :] = hi
-                    klo[k, a : a + block, :] = lo
+                    one, two = kf[2 * tau + 1 + odd, source], kf[2 * tau + 2 - odd, source]
+                hi, lo = split(jnp.concatenate([one, two], 0).T)
+                khi[k, :, tau * LANES : (tau + 1) * LANES] = hi
+                klo[k, :, tau * LANES : (tau + 1) * LANES] = lo
         return 0
 
     lax.fori_loop(0, pairs, prepare, 0)
@@ -309,9 +310,9 @@
                     made = []
                     for k in (2 * p, 2 * p + 1):
                         hi, lo = picked[k, :, :wide], picked[k, :, wide:]
-                        k_hi, k_lo = khi[k, start:stop, :], klo[k, start:stop, :]
+                        k_hi, k_lo = khi[k, :, start:stop], klo[k, :, start:stop]
                         made.append(
-                            dot_nt(jnp.concatenate([hi, lo, hi], 1), jnp.concatenate([k_hi, k_hi, k_lo], 1))
+                            dot_nn(jnp.concatenate([hi, lo, hi], 1), jnp.concatenate([k_hi, k_hi, k_lo], 0))
                         )
                     for piece in range(start, stop, LANES):
                         tau = piece // LANES
@@ -466,6 +467,15 @@
             coef_out[first + j : first + j + 1, :] = jnp.broadcast_to(a, (1, LANES))
 
 
+def combine(v0_ref, v1_ref, v2_ref, v3_ref, coef_ref, x_ref, r_ref):
+    basis = (v0_ref, v1_ref, v2_ref, v3_ref)
+    for q in range(0, v0_ref.shape[1], LANES):
+        at = slice(q, q + LANES)
+        parts = [v[:, at] for v in basis]
+        x_ref[:, at] = sum(coef_ref[j : j + 1, :] * parts[j] for j in range(ITERS))
+        r_ref[:, at] = sum(coef_ref[8 + j : 9 + j, :] * parts[j] for j in range(ITERS + 1))
+
+
 def per_device(right_side, diagonal, stiffness, columns, interface, triples, coupling_values):
     n_space, n_chaos = lax.axis_size("space"), lax.axis_size("chaos")
     modes, width = right_side.shape
@@ -488,12 +498,12 @@
     *basis, coefs = pl.pallas_call(
         functools.partial(kernel, n_space, n_chaos, stage),
         out_shape=(out,) * (ITERS + 1) + (jax.ShapeDtypeStruct((16, LANES), f32),),
-        in_specs=[vmem, vmem, pl.BlockSpec(memory_space=pl.ANY), smem, smem, vmem, vmem],
+        in_specs=[vmem, vmem, pl.BlockSpec(memory_space=pltpu.HBM), smem, smem, vmem, vmem],
         out_specs=(vmem,) * (ITERS + 2),
         scratch_shapes=[
             pltpu.VMEM(stiffness.shape, f32),
-            pltpu.VMEM((nbr, cols, depth), bf16),
-            pltpu.VMEM((nbr, cols, depth), bf16),
+            pltpu.VMEM((nbr, depth, cols), bf16),
+            pltpu.VMEM((nbr, depth, cols), bf16),
             pltpu.VMEM((2, mp, 3 * whole_depth), bf16),
             pltpu.VMEM((mp, LANES), f32),
             pltpu.VMEM((n_chaos, hp, width), f32),
@@ -522,16 +532,20 @@
             dma((stage,)), dma((stage,)), dma((n_group,)), dma((n_group,)),
         ],
         compiler_params=pltpu.CompilerParams(
-            collective_id=0, has_side_effects=True, vmem_limit_bytes=60 * 1024 * 1024
+            collective_id=0, has_side_effects=True, vmem_limit_bytes=56 * 1024 * 1024
         ),
         name="solve",
     )(
         right_side, diagonal, stiffness, columns.T, interface, triples.T,
         coupling_values,
     )
-    field = sum(coefs[j, 0] * basis[j] for j in range(ITERS))
-    residual = sum(coefs[8 + j, 0] * basis[j] for j in range(ITERS + 1))
-    return field, residual
+    return pl.pallas_call(
+        combine,
+        out_shape=(out, out),
+        in_specs=[vmem] * (ITERS + 2),
+        out_specs=(vmem, vmem),
+        name="combine",
+    )(*basis, coefs)
 
 
 def solution(mesh):

time: 44.9 us -> 38 us (0.85)
  other arithmetic: 6.24 us -> 0 us
  local copies, waits for them, and re-layouts: 1.43 us -> 0 us
  Pallas kernels: 36.4 us -> 37.2 us
    add x1 -> x0, other arithmetic: 6.24 us -> none  [per_device(): residual = sum((coefs[8 + j, 0] * basis[j] for j in range(ITERS + 1)))]
    pallas_call x0 -> x1, Pallas kernels: none -> 2.01 us  [per_device(): pl.pallas_call(combine, out_shape=(out, out), in_specs=[vmem] * (ITERS +...]
    slice x1 -> x0, local copies, waits for them, and re-layouts: 1.43 us -> none  [per_device(): residual = sum((coefs[8 + j, 0] * basis[j] for j in range(ITERS + 1)))]
    pallas_call x1, Pallas kernels: 36.4 us -> 35.2 us  [per_device(): pl.pallas_call(functools.partial(kernel, n_space, n_chaos, stage), out_sh...]
where the time goes in v3:
time: 38 us; the launch traced here: 37.9 us
  Pallas kernels  37.2 us (98%)
  between operations  0.64 us (2%)
    pallas_call x1, Pallas kernels, per_device(): pl.pallas_call(functools.partial(kernel, n_space, n_chaos, stage), out_sh...  35.2 us
    pallas_call x1, Pallas kernels, per_device(): pl.pallas_call(combine, out_shape=(out, out), in_specs=[vmem] * (ITERS +...  2.01 us

profile of v3, /device:TPU:0, one launch (start us, length us, event | category | flops | bytes accessed | tf_op | source)
XLA Modules:
  0.0 37.9 jit_solution(1746169190591463806)
XLA Ops:
  0.6 35.2 %solve.1 = (f32[84,512]{1,0:T(8,128)}, f32[84,512]{1,0:T(8,128)}, f32[84,512]{1,0:T(8,128)}, f32[84,512]{1,0:T(8,128)}, f32[16,128]{1,0:T(8,128)}) custom-call(f32[84,512]{1,0:T(8,128)} %b_ref.1, f32[84,512]{1,0:T(8,128)} %d_ref.1, f32[9,8,64,256]{3,2,1,0:T(8,128)} %k_hbm.1, s32[4,8]{1,0:T(4,128)} %bitcast.3, s32[1,2]{1,0:T(1,128)} %if_ref.1, ...), custom_call_target="tpu_custom_call" | custom-call | tf_op jit(solution)/shard_map/solve/pallas_call | solution.py:498
  35.9 2.0 %combine.1 = (f32[84,512]{1,0:T(8,128)}, f32[84,512]{1,0:T(8,128)}) custom-call(f32[84,512]{1,0:T(8,128)} %get-tuple-element.7.v0_ref, f32[84,512]{1,0:T(8,128)} %get-tuple-element.8.v1_ref, f32[84,512]{1,0:T(8,128)} %get-tuple-element.9.v2_ref, f32[84,512]{1,0:T(8,128)} %get-tuple-element.10.v3_ref, f32[16,128]{1,0:T(8,128)} %get-tuple-element.11.coef_ref), custom_call_target="tpu_custom_call" | custom-call | tf_op jit(solution)/shard_map/combine/pallas_call | solution.py:542

commit v4 on v3

--- a/solution.py
+++ b/solution.py
@@ -57,18 +57,18 @@
 
 
 def kernel(
-    n_space, n_chaos, stage,
+    n_space, n_chaos,
     b_ref, d_ref, k_hbm, col_ref, if_ref, tri_ref, val_ref,
     v0_out, v1_out, v2_out, v3_out, coef_out,
-    kf, khi, klo, c3, cdiag, gb, gd, nat, ef0, ef1, vec, dg, picked, rodd, reven,
-    own_send, own_blocks, halo0, halo_out, halo_in, stat, red1, red2, natv,
+    kf, khi, klo, c3, cdiag, gb, gd, ef0, ef1, vec, picked, rodd, reven,
+    own_send, own_blocks, halo0, halo_out, halo_in, stat, red, natv,
     k_sem, gb_send, gb_recv, gd_send, gd_recv, h0_send, h0_recv, h_send, h_recv,
-    r1_send, r1_recv, r2_send, r2_recv,
+    r_send, r_recv,
 ):
     f32 = jnp.float32
     modes, width = b_ref.shape
-    hp = gb.shape[1]
-    mp = n_chaos * hp
+    mp = gb.shape[1]
+    hp = mp // n_chaos
     terms, nbr, block, _ = kf.shape
     nnz = col_ref.shape[0]
     pairs = nbr // 2
@@ -82,8 +82,6 @@
     k_copy.start()
 
     barrier = pltpu.get_barrier_semaphore()
-    group, place = s // stage, s % stage
-    n_group = n_space // stage
     has_left, has_right = s > 0, s < n_space - 1
 
     def greet(space, chaos):
@@ -99,28 +97,48 @@
         @pl.when(has_right)
         def _():
             greet(s + 1, (c + d) % n_chaos)
-    for d in range(1, stage):
-        greet(group * stage + (place + d) % stage, c)
-    for d in range(1, n_group):
-        greet(((group + d) % n_group) * stage + place, c)
-
-    own_b = jnp.concatenate([b_ref[...], jnp.zeros((hp - modes, width), f32)], 0) if hp > modes else b_ref[...]
-    own_d = jnp.concatenate([d_ref[...], jnp.zeros((hp - modes, width), f32)], 0) if hp > modes else d_ref[...]
-    gb[c] = own_b
-    gd[c] = own_d
+    for d in range(1, n_space):
+        greet((s + d) % n_space, c)
+
+    if0, if1 = if_ref[0, 0], if_ref[0, 1]
+    second = jnp.where(if1 == if0, jnp.where(if0 == 0, 1, 0), if1)
+    small, large = jnp.minimum(if0, second), jnp.maximum(if0, second)
+
+    def block_at(k):
+        if isinstance(k, int) and k < 2:
+            return if0 if k == 0 else second
+        row = k - 2
+        row = row + one_way(row >= small)
+        return row + one_way(row >= large)
+
+    def place_of(row):
+        rest = 2 + row - one_way(if0 < row) - one_way(second < row)
+        found = jnp.where(row == if0, 0, jnp.where(row == second, 1, rest))
+        return jnp.where(row >= nbr, row, found)
+
+    mine = pl.ds(pl.multiple_of(c * hp, 8), hp)
     low_hp = low_half((hp, LANES))
-    for q in range(pairs):
-        chunk = own_b[:, q * LANES : (q + 1) * LANES]
-        turned = swap(chunk)
-        own_blocks[2 * q] = jnp.where(low_hp, chunk, turned)
-        own_blocks[2 * q + 1] = jnp.where(low_hp, turned, chunk)
-    if0, if1 = if_ref[0, 0], if_ref[0, 1]
-    own_send[1] = pack(own_blocks[if0])
-    own_send[0] = pack(own_blocks[if1])
+
+    def own_rows(ref, which, buf):
+        for q in range(pairs):
+            chunk = ref[:, q * LANES : (q + 1) * LANES]
+            if hp > modes:
+                chunk = jnp.concatenate([chunk, jnp.zeros((hp - modes, LANES), f32)], 0)
+            turned = swap(chunk)
+            own_blocks[which, 2 * q] = jnp.where(low_hp, chunk, turned)
+            own_blocks[which, 2 * q + 1] = jnp.where(low_hp, turned, chunk)
+        for p in range(pairs):
+            one, two = own_blocks[which, block_at(2 * p)], own_blocks[which, block_at(2 * p + 1)]
+            buf[p, mine, :] = jnp.where(low_hp, one, two)
+
+    own_rows(b_ref, 0, gb)
+    own_send[1] = pack(own_blocks[0, if0])
+    own_send[0] = pack(own_blocks[0, if1])
+    own_rows(d_ref, 1, gd)
 
     pl.semaphore_wait(
         barrier,
-        (n_chaos - 1) + n_chaos * (one_way(has_left) + one_way(has_right)) + (stage - 1) + (n_group - 1),
+        (n_chaos - 1) + n_chaos * (one_way(has_left) + one_way(has_right)) + (n_space - 1),
     )
 
     def halo0_copy(side, d):
@@ -130,12 +148,22 @@
             device_id=(s + 1 if side == 0 else s - 1, (c + d) % n_chaos), device_id_type=MESH,
         )
 
-    def gather_copy(buf, send, recv, d):
+    half_pairs = pairs // 2
+
+    def gather_copy(buf, part, send, recv, d):
+        which = buf.at[part, mine, :]
         return pltpu.make_async_remote_copy(
-            src_ref=buf.at[c], dst_ref=buf.at[c], send_sem=send.at[d], recv_sem=recv.at[d],
+            src_ref=which, dst_ref=which, send_sem=send, recv_sem=recv,
             device_id=(s, (c + d) % n_chaos), device_id_type=MESH,
         )
 
+    def b_copy(d):
+        return gather_copy(gb, pl.ds(0, pairs), gb_send.at[d], gb_recv.at[d], d)
+
+    def d_copy(half, d):
+        part = pl.ds(half * half_pairs, half_pairs)
+        return gather_copy(gd, part, gd_send.at[half, d], gd_recv.at[half, d], d)
+
     for d in range(n_chaos):
         @pl.when(has_right)
         def _():
@@ -145,24 +173,7 @@
         def _():
             halo0_copy(1, d).start()
     for d in range(1, n_chaos):
-        gather_copy(gb, gb_send, gb_recv, d).start()
-    for d in range(1, n_chaos):
-        gather_copy(gd, gd_send, gd_recv, d).start()
-
-    second = jnp.where(if1 == if0, jnp.where(if0 == 0, 1, 0), if1)
-    small, large = jnp.minimum(if0, second), jnp.maximum(if0, second)
-
-    def block_at(k):
-        if isinstance(k, int) and k < 2:
-            return if0 if k == 0 else second
-        row = k - 2
-        row = row + one_way(row >= small)
-        return row + one_way(row >= large)
-
-    def place_of(row):
-        rest = 2 + row - one_way(if0 < row) - one_way(second < row)
-        found = jnp.where(row == if0, 0, jnp.where(row == second, 1, rest))
-        return jnp.where(row >= nbr, row, found)
+        b_copy(d).start()
 
     def slot(mode):
         shift = jnp.zeros_like(mode)
@@ -187,8 +198,8 @@
     lanes_iota = lax.broadcasted_iota(jnp.int32, (LANES, depth), 1)
     for parity in range(2):
         first = 1 if parity == 0 else 2
-        mine = (term > 0) & ((term & 1) == (first & 1))
-        key = jnp.where(mine, ((term - first) >> 1) * mp + col, -1)
+        listed = (term > 0) & ((term & 1) == (first & 1))
+        key = jnp.where(listed, ((term - first) >> 1) * mp + col, -1)
         key = jnp.concatenate([key, jnp.full((1, padded - entries), -1, jnp.int32)], 1)
         hot = []
         for n in range(0, padded, LANES):
@@ -226,22 +237,15 @@
 
     low = low_half((mp, LANES))
 
-    def spread_blocks(buf):
-        for q in range(pairs):
-            for h in range(n_chaos):
-                chunk = buf[h, :, q * LANES : (q + 1) * LANES]
-                turned = swap(chunk)
-                nat[2 * q, h * hp : (h + 1) * hp] = jnp.where(low_hp, chunk, turned)
-                nat[2 * q + 1, h * hp : (h + 1) * hp] = jnp.where(low_hp, turned, chunk)
-
     for d in range(1, n_chaos):
-        gather_copy(gb, gb_send, gb_recv, d).wait()
-    spread_blocks(gb)
+        b_copy(d).wait()
+    for d in range(1, n_chaos):
+        d_copy(0, d).start()
     for p in range(pairs):
-        one, two = nat[block_at(2 * p)], nat[block_at(2 * p + 1)]
-        ef0[2 * p] = one
-        ef0[2 * p + 1] = two
-        vec[0, p] = jnp.where(low, one, two)
+        chunk = gb[p]
+        turned = swap(chunk)
+        ef0[2 * p] = jnp.where(low, chunk, turned)
+        ef0[2 * p + 1] = jnp.where(low, turned, chunk)
 
     def fill(side, now, read):
         present = has_left if side == 0 else has_right
@@ -284,10 +288,12 @@
         sums[(i, j)] = sums[(i, j)] + part if (i, j) in sums else part
 
     for p in range(pairs):
-        add_product(0, 0, vec[0, p], vec[0, p])
+        add_product(0, 0, gb[p], gb[p])
+
+    def basis(j, p, rows=slice(None)):
+        return gb[p, rows, :] if j == 0 else vec[j - 1, p, rows, :]
 
     scale0 = cdiag[...]
-    half_pairs = pairs // 2
     n_odd = even_terms * LANES
     wide = nnz * block
     for it in range(ITERS):
@@ -331,23 +337,22 @@
             for parity, rhs in ((0, rodd), (1, reven)):
                 hi, lo = rhs[half, 0], rhs[half, 1]
                 coupled.append(dot_nn(c3[parity], jnp.concatenate([hi, hi, lo], 0)))
-            if it == 0 and half == 0:
+            if it == 0:
                 for d in range(1, n_chaos):
-                    gather_copy(gd, gd_send, gd_recv, d).wait()
-                spread_blocks(gd)
-                for p in range(pairs):
-                    one, two = nat[block_at(2 * p)], nat[block_at(2 * p + 1)]
-                    dg[p] = jnp.where(low, one, two) - SHIFT
+                    d_copy(half, d).wait()
+                if half == 0:
+                    for d in range(1, n_chaos):
+                        d_copy(1, d).start()
             for step in range(half_pairs):
                 p = half * half_pairs + step
                 at = slice(step * LANES, (step + 1) * LANES)
                 new = coupled[0][:, at] + swap(coupled[1][:, at]) + scale0 * zeros[step]
-                new = dg[p] * vec[it, p] + new
+                new = (gd[p] - SHIFT) * basis(it, p) + new
                 if it > 0:
-                    new = new - GAMMA[it] * vec[it - 1, p]
-                vec[it + 1, p] = new
+                    new = new - GAMMA[it] * basis(it - 1, p)
+                vec[it, p] = new
                 for j in range(it + 1):
-                    add_product(j, it + 1, vec[j, p], new)
+                    add_product(j, it + 1, basis(j, p), new)
                 if it < ITERS - 1:
                     add_product(it + 1, it + 1, new, new)
                     turned = swap(new)
@@ -380,25 +385,20 @@
     for e, pair in enumerate(PAIRS):
         stat[e : e + 1, :] = jnp.sum(sums[pair], axis=0, keepdims=True)
 
-    def reduce_copy(level, d):
-        if level == 0:
-            target, src, dst, send, recv = group * stage + (place + d) % stage, stat, red1.at[place], r1_send, r1_recv
-        else:
-            target, src, dst, send, recv = ((group + d) % n_group) * stage + place, stat, red2.at[group], r2_send, r2_recv
+    def reduce_copy(d):
         return pltpu.make_async_remote_copy(
-            src_ref=src, dst_ref=dst, send_sem=send.at[d], recv_sem=recv.at[d],
-            device_id=(target, c), device_id_type=MESH,
+            src_ref=stat, dst_ref=red.at[s], send_sem=r_send.at[d], recv_sem=r_recv.at[d],
+            device_id=((s + d) % n_space, c), device_id_type=MESH,
         )
 
-    red1[place] = stat[...]
-    for d in range(1, stage):
-        reduce_copy(0, d).start()
-
-    mine = pl.ds(pl.multiple_of(c * hp, 8), hp)
+    for d in range(1, n_space):
+        reduce_copy(d).start()
+    red[s] = stat[...]
+
     back = [place_of(jnp.int32(k)) for k in range(nbr)]
     for j in range(ITERS + 1):
         for p in range(pairs):
-            chunk = vec[j, p, mine, :]
+            chunk = basis(j, p, mine)
             turned = swap(chunk)
             natv[j, 2 * p] = jnp.where(low_hp, chunk, turned)
             natv[j, 2 * p + 1] = jnp.where(low_hp, turned, chunk)
@@ -407,20 +407,11 @@
             chunk = jnp.where(low_hp, natv[j, back[2 * q]], natv[j, back[2 * q + 1]])
             out[:, q * LANES : (q + 1) * LANES] = chunk[:modes]
 
-    for d in range(1, stage):
-        reduce_copy(0, d).wait()
-    total = red1[0]
-    for g in range(1, stage):
-        total = total + red1[g]
-    stat[...] = total
-    red2[group] = total
-    for d in range(1, n_group):
-        reduce_copy(1, d).start()
-    for d in range(1, n_group):
-        reduce_copy(1, d).wait()
-    total = red2[0]
-    for g in range(1, n_group):
-        total = total + red2[g]
+    for d in range(1, n_space):
+        reduce_copy(d).wait()
+    total = red[0]
+    for g in range(1, n_space):
+        total = total + red[g]
     total = jnp.sum(total, axis=1, keepdims=True)
     gram = {}
     for e, (i, j) in enumerate(PAIRS):
@@ -485,10 +476,6 @@
     pairs = nbr // 2
     even_terms = (terms - 1) // 2
     cols = even_terms * LANES + 2 * block
-    stage = 1
-    while stage * stage < n_space:
-        stage *= 2
-    n_group = n_space // stage
     f32, bf16 = jnp.float32, jnp.bfloat16
     vmem = pl.BlockSpec(memory_space=pltpu.VMEM)
     smem = pl.BlockSpec(memory_space=pltpu.SMEM)
@@ -496,7 +483,7 @@
     out = jax.ShapeDtypeStruct((modes, width), f32)
     whole_depth = -(-even_terms * mp // 256) * 256
     *basis, coefs = pl.pallas_call(
-        functools.partial(kernel, n_space, n_chaos, stage),
+        functools.partial(kernel, n_space, n_chaos),
         out_shape=(out,) * (ITERS + 1) + (jax.ShapeDtypeStruct((16, LANES), f32),),
         in_specs=[vmem, vmem, pl.BlockSpec(memory_space=pltpu.HBM), smem, smem, vmem, vmem],
         out_specs=(vmem,) * (ITERS + 2),
@@ -506,30 +493,27 @@
             pltpu.VMEM((nbr, depth, cols), bf16),
             pltpu.VMEM((2, mp, 3 * whole_depth), bf16),
             pltpu.VMEM((mp, LANES), f32),
-            pltpu.VMEM((n_chaos, hp, width), f32),
-            pltpu.VMEM((n_chaos, hp, width), f32),
-            pltpu.VMEM((nbr, mp, LANES), f32),
+            pltpu.VMEM((pairs, mp, LANES), f32),
+            pltpu.VMEM((pairs, mp, LANES), f32),
             pltpu.VMEM((nbr + 2, mp, LANES), f32),
             pltpu.VMEM((nbr + 2, mp, LANES), f32),
-            pltpu.VMEM((ITERS + 1, pairs, mp, LANES), f32),
-            pltpu.VMEM((pairs, mp, LANES), f32),
+            pltpu.VMEM((ITERS, pairs, mp, LANES), f32),
             pltpu.VMEM((nbr, mp, 2 * depth), bf16),
             pltpu.VMEM((2, 2, whole_depth, pairs // 2 * LANES), bf16),
             pltpu.VMEM((2, 2, whole_depth, pairs // 2 * LANES), bf16),
             pltpu.VMEM((2, packed_rows(hp), LANES), f32),
-            pltpu.VMEM((nbr, hp, LANES), f32),
+            pltpu.VMEM((2, nbr, hp, LANES), f32),
             pltpu.VMEM((2, n_chaos, packed_rows(hp), LANES), f32),
             pltpu.VMEM((ITERS - 1, 2, packed_rows(mp), LANES), f32),
             pltpu.VMEM((ITERS - 1, 2, packed_rows(mp), LANES), f32),
             pltpu.VMEM((16, LANES), f32),
-            pltpu.VMEM((stage, 16, LANES), f32),
-            pltpu.VMEM((n_group, 16, LANES), f32),
+            pltpu.VMEM((n_space, 16, LANES), f32),
             pltpu.VMEM((ITERS + 1, nbr, hp, LANES), f32),
             dma,
-            dma((n_chaos,)), dma((n_chaos,)), dma((n_chaos,)), dma((n_chaos,)),
+            dma((n_chaos,)), dma((n_chaos,)), dma((2, n_chaos)), dma((2, n_chaos)),
             dma((2, n_chaos)), dma((2, n_chaos)),
             dma((ITERS - 1, 2)), dma((ITERS - 1, 2)),
-            dma((stage,)), dma((stage,)), dma((n_group,)), dma((n_group,)),
+            dma((n_space,)), dma((n_space,)),
         ],
         compiler_params=pltpu.CompilerParams(
             collective_id=0, has_side_effects=True, vmem_limit_bytes=56 * 1024 * 1024

time: 38 us -> 36.9 us (0.971)
  Pallas kernels: 37.2 us -> 36.1 us
    pallas_call x1, Pallas kernels: 35.2 us -> 34.1 us  [per_device(): pl.pallas_call(functools.partial(kernel, n_space, n_chaos), out_shape=(ou...]
where the time goes in v4:
time: 36.9 us; the launch traced here: 36.7 us
  Pallas kernels  36.1 us (98%)
  between operations  0.64 us (2%)
    pallas_call x1, Pallas kernels, per_device(): pl.pallas_call(functools.partial(kernel, n_space, n_chaos), out_shape=(ou...  34.1 us
    pallas_call x1, Pallas kernels, per_device(): pl.pallas_call(combine, out_shape=(out, out), in_specs=[vmem] * (ITERS +...  2.01 us

profile of v4, /device:TPU:0, one launch (start us, length us, event | category | flops | bytes accessed | tf_op | source)
XLA Modules:
  0.0 36.7 jit_solution(11286126135059400516)
XLA Ops:
  0.6 34.1 %solve.1 = (f32[84,512]{1,0:T(8,128)}, f32[84,512]{1,0:T(8,128)}, f32[84,512]{1,0:T(8,128)}, f32[84,512]{1,0:T(8,128)}, f32[16,128]{1,0:T(8,128)}) custom-call(f32[84,512]{1,0:T(8,128)} %b_ref.1, f32[84,512]{1,0:T(8,128)} %d_ref.1, f32[9,8,64,256]{3,2,1,0:T(8,128)} %k_hbm.1, s32[4,8]{1,0:T(4,128)} %bitcast.3, s32[1,2]{1,0:T(1,128)} %if_ref.1, ...), custom_call_target="tpu_custom_call" | custom-call | tf_op jit(solution)/shard_map/solve/pallas_call | solution.py:485
  34.7 2.0 %combine.1 = (f32[84,512]{1,0:T(8,128)}, f32[84,512]{1,0:T(8,128)}) custom-call(f32[84,512]{1,0:T(8,128)} %get-tuple-element.7.v0_ref, f32[84,512]{1,0:T(8,128)} %get-tuple-element.8.v1_ref, f32[84,512]{1,0:T(8,128)} %get-tuple-element.9.v2_ref, f32[84,512]{1,0:T(8,128)} %get-tuple-element.10.v3_ref, f32[16,128]{1,0:T(8,128)} %get-tuple-element.11.coef_ref), custom_call_target="tpu_custom_call" | custom-call | tf_op jit(solution)/shard_map/combine/pallas_call | solution.py:526

commit v5 on v4

--- a/solution.py
+++ b/solution.py
@@ -59,8 +59,8 @@
 def kernel(
     n_space, n_chaos,
     b_ref, d_ref, k_hbm, col_ref, if_ref, tri_ref, val_ref,
-    v0_out, v1_out, v2_out, v3_out, coef_out,
-    kf, khi, klo, c3, cdiag, gb, gd, ef0, ef1, vec, picked, rodd, reven,
+    basis_out, coef_out,
+    kf, khi, klo, c3, cdiag, gb, gd, ef, vec, picked, rodd, reven,
     own_send, own_blocks, halo0, halo_out, halo_in, stat, red, natv,
     k_sem, gb_send, gb_recv, gd_send, gd_recv, h0_send, h0_recv, h_send, h_recv,
     r_send, r_recv,
@@ -73,8 +73,7 @@
     nnz = col_ref.shape[0]
     pairs = nbr // 2
     even_terms = (terms - 1) // 2
-    depth = rodd.shape[2]
-    ef = (ef0, ef1)
+    depth = rodd.shape[1]
     s = lax.axis_index("space")
     c = lax.axis_index("chaos")
 
@@ -109,7 +108,8 @@
             return if0 if k == 0 else second
         row = k - 2
         row = row + one_way(row >= small)
-        return row + one_way(row >= large)
+        row = row + one_way(row >= large)
+        return row if isinstance(k, int) else jnp.where(k == 0, if0, jnp.where(k == 1, second, row))
 
     def place_of(row):
         rest = 2 + row - one_way(if0 < row) - one_way(second < row)
@@ -196,9 +196,10 @@
     padded = -(-entries // LANES) * LANES
     spread2 = jnp.concatenate([spread2, jnp.zeros((2 * mp, padded - entries), spread2.dtype)], 1)
     lanes_iota = lax.broadcasted_iota(jnp.int32, (LANES, depth), 1)
-    for parity in range(2):
-        first = 1 if parity == 0 else 2
-        listed = (term > 0) & ((term & 1) == (first & 1))
+
+    def table(parity, _):
+        first = 1 + parity
+        listed = (term > 0) & ((term & 1) == 1 - parity)
         key = jnp.where(listed, ((term - first) >> 1) * mp + col, -1)
         key = jnp.concatenate([key, jnp.full((1, padded - entries), -1, jnp.int32)], 1)
         hot = []
@@ -210,19 +211,21 @@
         c3[parity, :, :depth] = both[:mp]
         c3[parity, :, depth : 2 * depth] = both[mp:]
         c3[parity, :, 2 * depth :] = both[:mp]
+        return 0
+
+    lax.fori_loop(0, 2, table, 0)
     if depth > even_terms * mp:
-        rest = jnp.zeros((depth - even_terms * mp, rodd.shape[3]), jnp.bfloat16)
-        for half in range(2):
-            for part in range(2):
-                rodd[half, part, even_terms * mp :, :] = rest
-                reven[half, part, even_terms * mp :, :] = rest
+        rest = jnp.zeros((depth - even_terms * mp, rodd.shape[2]), jnp.bfloat16)
+        for part in range(2):
+            rodd[part, even_terms * mp :, :] = rest
+            reven[part, even_terms * mp :, :] = rest
 
     k_copy.wait()
 
     def prepare(j, _):
         for odd in range(2):
             k = 2 * j + odd
-            source = jnp.where(k == 0, if0, jnp.where(k == 1, second, block_at(k)))
+            source = block_at(k)
             for tau in range(even_terms + 1):
                 if tau == even_terms:
                     one = two = kf[0, source]
@@ -244,8 +247,9 @@
     for p in range(pairs):
         chunk = gb[p]
         turned = swap(chunk)
-        ef0[2 * p] = jnp.where(low, chunk, turned)
-        ef0[2 * p + 1] = jnp.where(low, turned, chunk)
+        vec[0, p] = chunk
+        ef[0, 2 * p] = jnp.where(low, chunk, turned)
+        ef[0, 2 * p + 1] = jnp.where(low, turned, chunk)
 
     def fill(side, now, read):
         present = has_left if side == 0 else has_right
@@ -256,14 +260,14 @@
 
         @pl.when(jnp.logical_not(present))
         def _():
-            ef[now][nbr + side] = jnp.zeros((mp, LANES), f32)
+            ef[now, nbr + side] = jnp.zeros((mp, LANES), f32)
 
     for side in range(2):
         def read_first():
             for d in range(n_chaos):
                 halo0_copy(side, d).wait_recv()
             for h in range(n_chaos):
-                ef0[nbr + side, h * hp : (h + 1) * hp] = unpack(halo0[side, h], hp)
+                ef[0, nbr + side, h * hp : (h + 1) * hp] = unpack(halo0[side, h], hp)
 
         fill(side, 0, read_first)
     for side in range(2):
@@ -279,101 +283,101 @@
             device_id=(s + 1 if side == 0 else s - 1, c), device_id_type=MESH,
         )
 
-    places = [[place_of(col_ref[n, block_at(k)]) for n in range(nnz)] for k in range(nbr)]
     right_place = place_of(if1)
-    sums = {}
-
-    def add_product(i, j, one, two):
-        part = jnp.sum((one * two).reshape(mp // 8, 8, LANES), axis=0)
-        sums[(i, j)] = sums[(i, j)] + part if (i, j) in sums else part
-
-    for p in range(pairs):
-        add_product(0, 0, gb[p], gb[p])
-
-    def basis(j, p, rows=slice(None)):
-        return gb[p, rows, :] if j == 0 else vec[j - 1, p, rows, :]
-
     scale0 = cdiag[...]
     n_odd = even_terms * LANES
     wide = nnz * block
-    for it in range(ITERS):
-        now, later = it % 2, (it + 1) % 2
-        for half in range(2):
-            zeros = []
-            for step in range(half_pairs):
-                p = half * half_pairs + step
-                for k in (2 * p, 2 * p + 1):
-                    at = places[k]
-                    for m in range(nnz // 2):
-                        hi, lo = split(jnp.where(low, ef[now][at[2 * m]], ef[now][at[2 * m + 1]]))
-                        picked[k, :, m * LANES : (m + 1) * LANES] = hi
-                        picked[k, :, wide + m * LANES : wide + (m + 1) * LANES] = lo
-            for step in range(half_pairs):
-                p = half * half_pairs + step
-                to = pl.ds(step * LANES, LANES)
-                for start in range(0, n_odd + 2 * block, 2 * LANES):
-                    stop = min(start + 2 * LANES, n_odd + 2 * block)
-                    made = []
-                    for k in (2 * p, 2 * p + 1):
-                        hi, lo = picked[k, :, :wide], picked[k, :, wide:]
-                        k_hi, k_lo = khi[k, :, start:stop], klo[k, :, start:stop]
-                        made.append(
-                            dot_nn(jnp.concatenate([hi, lo, hi], 1), jnp.concatenate([k_hi, k_hi, k_lo], 0))
-                        )
-                    for piece in range(start, stop, LANES):
-                        tau = piece // LANES
-                        a = made[0][:, piece - start : piece - start + LANES]
-                        b = made[1][:, piece - start : piece - start + LANES]
-                        if piece == n_odd:
-                            zeros.append(jnp.where(low, a, b))
-                            continue
-                        hi, lo = split(jnp.where(low, a, b))
-                        rodd[half, 0, tau * mp : (tau + 1) * mp, to] = hi
-                        rodd[half, 1, tau * mp : (tau + 1) * mp, to] = lo
-                        hi, lo = split(jnp.where(low, b, a))
-                        reven[half, 0, tau * mp : (tau + 1) * mp, to] = hi
-                        reven[half, 1, tau * mp : (tau + 1) * mp, to] = lo
-            coupled = []
-            for parity, rhs in ((0, rodd), (1, reven)):
-                hi, lo = rhs[half, 0], rhs[half, 1]
-                coupled.append(dot_nn(c3[parity], jnp.concatenate([hi, hi, lo], 0)))
-            if it == 0:
+    per_half = 2 * half_pairs
+
+    def half_step(it, half):
+        now = it % 2
+        later = 1 - now
+        for i in range(per_half):
+            row = block_at(half * per_half + i)
+            at = [place_of(col_ref[n, row]) for n in range(nnz)]
+            for m in range(nnz // 2):
+                hi, lo = split(jnp.where(low, ef[now, at[2 * m]], ef[now, at[2 * m + 1]]))
+                picked[i, :, m * LANES : (m + 1) * LANES] = hi
+                picked[i, :, wide + m * LANES : wide + (m + 1) * LANES] = lo
+        zeros = []
+        for step in range(half_pairs):
+            to = pl.ds(step * LANES, LANES)
+            for start in range(0, n_odd + 2 * block, 2 * LANES):
+                stop = min(start + 2 * LANES, n_odd + 2 * block)
+                made = []
+                for i in (2 * step, 2 * step + 1):
+                    k = half * per_half + i
+                    hi, lo = picked[i, :, :wide], picked[i, :, wide:]
+                    k_hi, k_lo = khi[k, :, start:stop], klo[k, :, start:stop]
+                    made.append(
+                        dot_nn(jnp.concatenate([hi, lo, hi], 1), jnp.concatenate([k_hi, k_hi, k_lo], 0))
+                    )
+                for piece in range(start, stop, LANES):
+                    tau = piece // LANES
+                    a = made[0][:, piece - start : piece - start + LANES]
+                    b = made[1][:, piece - start : piece - start + LANES]
+                    if piece == n_odd:
+                        zeros.append(jnp.where(low, a, b))
+                        continue
+                    hi, lo = split(jnp.where(low, a, b))
+                    rodd[0, tau * mp : (tau + 1) * mp, to] = hi
+                    rodd[1, tau * mp : (tau + 1) * mp, to] = lo
+                    hi, lo = split(jnp.where(low, b, a))
+                    reven[0, tau * mp : (tau + 1) * mp, to] = hi
+                    reven[1, tau * mp : (tau + 1) * mp, to] = lo
+        coupled = []
+        for parity, rhs in ((0, rodd), (1, reven)):
+            hi, lo = rhs[0], rhs[1]
+            coupled.append(dot_nn(c3[parity], jnp.concatenate([hi, hi, lo], 0)))
+
+        @pl.when(it == 0)
+        def _():
+            for d in range(1, n_chaos):
+                d_copy(half, d).wait()
+
+            @pl.when(half == 0)
+            def _():
                 for d in range(1, n_chaos):
-                    d_copy(half, d).wait()
-                if half == 0:
-                    for d in range(1, n_chaos):
-                        d_copy(1, d).start()
-            for step in range(half_pairs):
-                p = half * half_pairs + step
-                at = slice(step * LANES, (step + 1) * LANES)
-                new = coupled[0][:, at] + swap(coupled[1][:, at]) + scale0 * zeros[step]
-                new = (gd[p] - SHIFT) * basis(it, p) + new
-                if it > 0:
-                    new = new - GAMMA[it] * basis(it - 1, p)
-                vec[it, p] = new
-                for j in range(it + 1):
-                    add_product(j, it + 1, basis(j, p), new)
-                if it < ITERS - 1:
-                    add_product(it + 1, it + 1, new, new)
-                    turned = swap(new)
-                    ef[later][2 * p] = jnp.where(low, new, turned)
-                    ef[later][2 * p + 1] = jnp.where(low, turned, new)
-            if it < ITERS - 1 and half == 0:
-                halo_out[it, 1] = pack(ef[later][0])
-                halo_out[it, 0] = pack(ef[later][right_place])
-
-                @pl.when(has_right)
-                def _():
-                    halo_copy(it, 0).start()
-
-                @pl.when(has_left)
-                def _():
-                    halo_copy(it, 1).start()
-        if it < ITERS - 1:
+                    d_copy(1, d).start()
+
+        gamma = jnp.where(it == 1, GAMMA[1], jnp.where(it == 2, GAMMA[2], GAMMA[0])).astype(f32)
+        for step in range(half_pairs):
+            p = half * half_pairs + step
+            at = slice(step * LANES, (step + 1) * LANES)
+            new = coupled[0][:, at] + swap(coupled[1][:, at]) + scale0 * zeros[step]
+            new = (gd[p] - SHIFT) * vec[it, p] + new - gamma * vec[jnp.maximum(it - 1, 0), p]
+            vec[it + 1, p] = new
+            turned = swap(new)
+            ef[later, 2 * p] = jnp.where(low, new, turned)
+            ef[later, 2 * p + 1] = jnp.where(low, turned, new)
+
+        @pl.when((half == 0) & (it < ITERS - 1))
+        def _():
+            halo_out[it, 1] = pack(ef[later, 0])
+            halo_out[it, 0] = pack(ef[later, right_place])
+
+            @pl.when(has_right)
+            def _():
+                halo_copy(it, 0).start()
+
+            @pl.when(has_left)
+            def _():
+                halo_copy(it, 1).start()
+
+    def iteration(it, _):
+        def one_half(half, _):
+            half_step(it, half)
+            return 0
+
+        lax.fori_loop(0, 2, one_half, 0)
+
+        @pl.when(it < ITERS - 1)
+        def _():
+            later = 1 - it % 2
             for side in range(2):
                 def read_next():
                     halo_copy(it, side).wait_recv()
-                    ef[later][nbr + side] = unpack(halo_in[it, side], mp)
+                    ef[later, nbr + side] = unpack(halo_in[it, side], mp)
 
                 fill(side, later, read_next)
             for side in range(2):
@@ -381,9 +385,22 @@
                 def _():
                     halo_copy(it, side).wait_send()
 
+        return 0
+
+    lax.fori_loop(0, ITERS, iteration, 0)
+
+    def products(p, sums):
+        parts = [vec[j, p] for j in range(ITERS + 1)]
+        return tuple(
+            total + jnp.sum((parts[i] * parts[j]).reshape(mp // 8, 8, LANES), axis=0)
+            for total, (i, j) in zip(sums, PAIRS)
+        )
+
+    sums = lax.fori_loop(0, pairs, products, tuple(jnp.zeros((8, LANES), f32) for _ in PAIRS))
+
     stat[...] = jnp.zeros_like(stat)
-    for e, pair in enumerate(PAIRS):
-        stat[e : e + 1, :] = jnp.sum(sums[pair], axis=0, keepdims=True)
+    for e, part in enumerate(sums):
+        stat[e : e + 1, :] = jnp.sum(part, axis=0, keepdims=True)
 
     def reduce_copy(d):
         return pltpu.make_async_remote_copy(
@@ -396,16 +413,19 @@
     red[s] = stat[...]
 
     back = [place_of(jnp.int32(k)) for k in range(nbr)]
-    for j in range(ITERS + 1):
+
+    def restore(j, _):
         for p in range(pairs):
-            chunk = basis(j, p, mine)
+            chunk = vec[j, p, mine, :]
             turned = swap(chunk)
-            natv[j, 2 * p] = jnp.where(low_hp, chunk, turned)
-            natv[j, 2 * p + 1] = jnp.where(low_hp, turned, chunk)
-    for j, out in enumerate((v0_out, v1_out, v2_out, v3_out)):
+            natv[2 * p] = jnp.where(low_hp, chunk, turned)
+            natv[2 * p + 1] = jnp.where(low_hp, turned, chunk)
         for q in range(pairs):
-            chunk = jnp.where(low_hp, natv[j, back[2 * q]], natv[j, back[2 * q + 1]])
-            out[:, q * LANES : (q + 1) * LANES] = chunk[:modes]
+            chunk = jnp.where(low_hp, natv[back[2 * q]], natv[back[2 * q + 1]])
+            basis_out[j, :, q * LANES : (q + 1) * LANES] = chunk[:modes]
+        return 0
+
+    lax.fori_loop(0, ITERS + 1, restore, 0)
 
     for d in range(1, n_space):
         reduce_copy(d).wait()
@@ -458,11 +478,10 @@
             coef_out[first + j : first + j + 1, :] = jnp.broadcast_to(a, (1, LANES))
 
 
-def combine(v0_ref, v1_ref, v2_ref, v3_ref, coef_ref, x_ref, r_ref):
-    basis = (v0_ref, v1_ref, v2_ref, v3_ref)
-    for q in range(0, v0_ref.shape[1], LANES):
+def combine(basis_ref, coef_ref, x_ref, r_ref):
+    for q in range(0, x_ref.shape[1], LANES):
         at = slice(q, q + LANES)
-        parts = [v[:, at] for v in basis]
+        parts = [basis_ref[j, :, at] for j in range(ITERS + 1)]
         x_ref[:, at] = sum(coef_ref[j : j + 1, :] * parts[j] for j in range(ITERS))
         r_ref[:, at] = sum(coef_ref[8 + j : 9 + j, :] * parts[j] for j in range(ITERS + 1))
 
@@ -482,11 +501,14 @@
     dma = pltpu.SemaphoreType.DMA
     out = jax.ShapeDtypeStruct((modes, width), f32)
     whole_depth = -(-even_terms * mp // 256) * 256
-    *basis, coefs = pl.pallas_call(
+    basis, coefs = pl.pallas_call(
         functools.partial(kernel, n_space, n_chaos),
-        out_shape=(out,) * (ITERS + 1) + (jax.ShapeDtypeStruct((16, LANES), f32),),
+        out_shape=(
+            jax.ShapeDtypeStruct((ITERS + 1, modes, width), f32),
+            jax.ShapeDtypeStruct((16, LANES), f32),
+        ),
         in_specs=[vmem, vmem, pl.BlockSpec(memory_space=pltpu.HBM), smem, smem, vmem, vmem],
-        out_specs=(vmem,) * (ITERS + 2),
+        out_specs=(vmem, vmem),
         scratch_shapes=[
             pltpu.VMEM(stiffness.shape, f32),
             pltpu.VMEM((nbr, depth, cols), bf16),
@@ -495,12 +517,11 @@
             pltpu.VMEM((mp, LANES), f32),
             pltpu.VMEM((pairs, mp, LANES), f32),
             pltpu.VMEM((pairs, mp, LANES), f32),
-            pltpu.VMEM((nbr + 2, mp, LANES), f32),
-            pltpu.VMEM((nbr + 2, mp, LANES), f32),
-            pltpu.VMEM((ITERS, pairs, mp, LANES), f32),
-            pltpu.VMEM((nbr, mp, 2 * depth), bf16),
-            pltpu.VMEM((2, 2, whole_depth, pairs // 2 * LANES), bf16),
-            pltpu.VMEM((2, 2, whole_depth, pairs // 2 * LANES), bf16),
+            pltpu.VMEM((2, nbr + 2, mp, LANES), f32),
+            pltpu.VMEM((ITERS + 1, pairs, mp, LANES), f32),
+            pltpu.VMEM((nbr // 2, mp, 2 * depth), bf16),
+            pltpu.VMEM((2, whole_depth, pairs // 2 * LANES), bf16),
+            pltpu.VMEM((2, whole_depth, pairs // 2 * LANES), bf16),
             pltpu.VMEM((2, packed_rows(hp), LANES), f32),
             pltpu.VMEM((2, nbr, hp, LANES), f32),
             pltpu.VMEM((2, n_chaos, packed_rows(hp), LANES), f32),
@@ -508,7 +529,7 @@
             pltpu.VMEM((ITERS - 1, 2, packed_rows(mp), LANES), f32),
             pltpu.VMEM((16, LANES), f32),
             pltpu.VMEM((n_space, 16, LANES), f32),
-            pltpu.VMEM((ITERS + 1, nbr, hp, LANES), f32),
+            pltpu.VMEM((nbr, hp, LANES), f32),
             dma,
             dma((n_chaos,)), dma((n_chaos,)), dma((2, n_chaos)), dma((2, n_chaos)),
             dma((2, n_chaos)), dma((2, n_chaos)),
@@ -526,10 +547,10 @@
     return pl.pallas_call(
         combine,
         out_shape=(out, out),
-        in_specs=[vmem] * (ITERS + 2),
+        in_specs=[vmem, vmem],
         out_specs=(vmem, vmem),
         name="combine",
-    )(*basis, coefs)
+    )(basis, coefs)
 
 
 def solution(mesh):

time: 36.9 us -> 37.7 us (1.022)
  Pallas kernels: 36.1 us -> 36.9 us
    pallas_call x2, Pallas kernels: 36.1 us -> 36.9 us  [the longest x1 34.9 us: per_device(): pl.pallas_call(functools.partial(kernel, n_space, n_chaos), out_shape=(ja...]
where the time goes in v5:
time: 37.7 us; the launch traced here: 37.5 us
  Pallas kernels  36.9 us (98%)
  between operations  0.64 us (2%)
    pallas_call x1, Pallas kernels, per_device(): pl.pallas_call(functools.partial(kernel, n_space, n_chaos), out_shape=(ja...  34.9 us
    pallas_call x1, Pallas kernels, per_device(): pl.pallas_call(combine, out_shape=(out, out), in_specs=[vmem, vmem], out_...  1.93 us

profile of v5, /device:TPU:0, one launch (start us, length us, event | category | flops | bytes accessed | tf_op | source)
XLA Modules:
  0.0 37.5 jit_solution(8195054300699572671)
XLA Ops:
  0.6 34.9 %solve.1 = (f32[4,84,512]{2,1,0:T(8,128)}, f32[16,128]{1,0:T(8,128)}) custom-call(f32[84,512]{1,0:T(8,128)} %b_ref.1, f32[84,512]{1,0:T(8,128)} %d_ref.1, f32[9,8,64,256]{3,2,1,0:T(8,128)} %k_hbm.1, s32[4,8]{1,0:T(4,128)} %bitcast.3, s32[1,2]{1,0:T(1,128)} %if_ref.1, s32[3,885]{1,0:T(4,128)} %bitcast.2, f32[885]{0:T(1024)} %val_ref.1), custom_call_target="tpu_custom_call" | custom-call | tf_op jit(solution)/shard_map/solve/pallas_call | solution.py:504
  35.6 1.9 %combine.1 = (f32[84,512]{1,0:T(8,128)}, f32[84,512]{1,0:T(8,128)}) custom-call(f32[4,84,512]{2,1,0:T(8,128)} %get-tuple-element.4.basis_ref, f32[16,128]{1,0:T(8,128)} %get-tuple-element.5.coef_ref), custom_call_target="tpu_custom_call" | custom-call | tf_op jit(solution)/shard_map/combine/pallas_call | solution.py:547

commit v6 on v5

--- a/solution.py
+++ b/solution.py
@@ -197,7 +197,7 @@
     spread2 = jnp.concatenate([spread2, jnp.zeros((2 * mp, padded - entries), spread2.dtype)], 1)
     lanes_iota = lax.broadcasted_iota(jnp.int32, (LANES, depth), 1)
 
-    def table(parity, _):
+    def table(parity):
         first = 1 + parity
         listed = (term > 0) & ((term & 1) == 1 - parity)
         key = jnp.where(listed, ((term - first) >> 1) * mp + col, -1)
@@ -211,9 +211,7 @@
         c3[parity, :, :depth] = both[:mp]
         c3[parity, :, depth : 2 * depth] = both[mp:]
         c3[parity, :, 2 * depth :] = both[:mp]
-        return 0
-
-    lax.fori_loop(0, 2, table, 0)
+
     if depth > even_terms * mp:
         rest = jnp.zeros((depth - even_terms * mp, rodd.shape[2]), jnp.bfloat16)
         for part in range(2):
@@ -222,7 +220,7 @@
 
     k_copy.wait()
 
-    def prepare(j, _):
+    def prepare(j):
         for odd in range(2):
             k = 2 * j + odd
             source = block_at(k)
@@ -234,9 +232,11 @@
                 hi, lo = split(jnp.concatenate([one, two], 0).T)
                 khi[k, :, tau * LANES : (tau + 1) * LANES] = hi
                 klo[k, :, tau * LANES : (tau + 1) * LANES] = lo
-        return 0
-
-    lax.fori_loop(0, pairs, prepare, 0)
+
+    for parity in range(2):
+        table(parity)
+        for j in range(parity * half_pairs, pairs if parity else half_pairs):
+            prepare(j)
 
     low = low_half((mp, LANES))
 
@@ -289,16 +289,17 @@
     wide = nnz * block
     per_half = 2 * half_pairs
 
-    def half_step(it, half):
-        now = it % 2
-        later = 1 - now
-        for i in range(per_half):
-            row = block_at(half * per_half + i)
+    def pick(it):
+        for k in range(nbr):
+            row = block_at(k)
             at = [place_of(col_ref[n, row]) for n in range(nnz)]
             for m in range(nnz // 2):
-                hi, lo = split(jnp.where(low, ef[now, at[2 * m]], ef[now, at[2 * m + 1]]))
-                picked[i, :, m * LANES : (m + 1) * LANES] = hi
-                picked[i, :, wide + m * LANES : wide + (m + 1) * LANES] = lo
+                hi, lo = split(jnp.where(low, ef[it % 2, at[2 * m]], ef[it % 2, at[2 * m + 1]]))
+                picked[k, :, m * LANES : (m + 1) * LANES] = hi
+                picked[k, :, wide + m * LANES : wide + (m + 1) * LANES] = lo
+
+    def half_step(it, half):
+        later = 1 - it % 2
         zeros = []
         for step in range(half_pairs):
             to = pl.ds(step * LANES, LANES)
@@ -307,7 +308,7 @@
                 made = []
                 for i in (2 * step, 2 * step + 1):
                     k = half * per_half + i
-                    hi, lo = picked[i, :, :wide], picked[i, :, wide:]
+                    hi, lo = picked[k, :, :wide], picked[k, :, wide:]
                     k_hi, k_lo = khi[k, :, start:stop], klo[k, :, start:stop]
                     made.append(
                         dot_nn(jnp.concatenate([hi, lo, hi], 1), jnp.concatenate([k_hi, k_hi, k_lo], 0))
@@ -330,29 +331,27 @@
             hi, lo = rhs[0], rhs[1]
             coupled.append(dot_nn(c3[parity], jnp.concatenate([hi, hi, lo], 0)))
 
-        @pl.when(it == 0)
-        def _():
+        if it == 0:
             for d in range(1, n_chaos):
                 d_copy(half, d).wait()
-
-            @pl.when(half == 0)
-            def _():
+            if half == 0:
                 for d in range(1, n_chaos):
                     d_copy(1, d).start()
 
-        gamma = jnp.where(it == 1, GAMMA[1], jnp.where(it == 2, GAMMA[2], GAMMA[0])).astype(f32)
         for step in range(half_pairs):
             p = half * half_pairs + step
             at = slice(step * LANES, (step + 1) * LANES)
             new = coupled[0][:, at] + swap(coupled[1][:, at]) + scale0 * zeros[step]
-            new = (gd[p] - SHIFT) * vec[it, p] + new - gamma * vec[jnp.maximum(it - 1, 0), p]
+            new = (gd[p] - SHIFT) * vec[it, p] + new
+            if it > 0:
+                new = new - GAMMA[it] * vec[it - 1, p]
             vec[it + 1, p] = new
-            turned = swap(new)
-            ef[later, 2 * p] = jnp.where(low, new, turned)
-            ef[later, 2 * p + 1] = jnp.where(low, turned, new)
-
-        @pl.when((half == 0) & (it < ITERS - 1))
-        def _():
+            if it < ITERS - 1:
+                turned = swap(new)
+                ef[later, 2 * p] = jnp.where(low, new, turned)
+                ef[later, 2 * p + 1] = jnp.where(low, turned, new)
+
+        if half == 0 and it < ITERS - 1:
             halo_out[it, 1] = pack(ef[later, 0])
             halo_out[it, 0] = pack(ef[later, right_place])
 
@@ -364,15 +363,11 @@
             def _():
                 halo_copy(it, 1).start()
 
-    def iteration(it, _):
-        def one_half(half, _):
+    for it in range(ITERS):
+        pick(it)
+        for half in range(2):
             half_step(it, half)
-            return 0
-
-        lax.fori_loop(0, 2, one_half, 0)
-
-        @pl.when(it < ITERS - 1)
-        def _():
+        if it < ITERS - 1:
             later = 1 - it % 2
             for side in range(2):
                 def read_next():
@@ -384,10 +379,6 @@
                 @pl.when(has_right if side == 0 else has_left)
                 def _():
                     halo_copy(it, side).wait_send()
-
-        return 0
-
-    lax.fori_loop(0, ITERS, iteration, 0)
 
     def products(p, sums):
         parts = [vec[j, p] for j in range(ITERS + 1)]
@@ -519,7 +510,7 @@
             pltpu.VMEM((pairs, mp, LANES), f32),
             pltpu.VMEM((2, nbr + 2, mp, LANES), f32),
             pltpu.VMEM((ITERS + 1, pairs, mp, LANES), f32),
-            pltpu.VMEM((nbr // 2, mp, 2 * depth), bf16),
+            pltpu.VMEM((nbr, mp, 2 * depth), bf16),
             pltpu.VMEM((2, whole_depth, pairs // 2 * LANES), bf16),
             pltpu.VMEM((2, whole_depth, pairs // 2 * LANES), bf16),
             pltpu.VMEM((2, packed_rows(hp), LANES), f32),

time: 37.7 us -> 37.2 us (0.987)
  Pallas kernels: 36.9 us -> 36.5 us
    pallas_call x1, Pallas kernels: 34.9 us -> 34.5 us  [per_device(): pl.pallas_call(functools.partial(kernel, n_space, n_chaos), out_shape=(ja...]
where the time goes in v6:
time: 37.2 us; the launch traced here: 37.1 us
  Pallas kernels  36.5 us (98%)
  between operations  0.64 us (2%)
    pallas_call x1, Pallas kernels, per_device(): pl.pallas_call(functools.partial(kernel, n_space, n_chaos), out_shape=(ja...  34.5 us
    pallas_call x1, Pallas kernels, per_device(): pl.pallas_call(combine, out_shape=(out, out), in_specs=[vmem, vmem], out_...  1.93 us

profile of v6, /device:TPU:0, one launch (start us, length us, event | category | flops | bytes accessed | tf_op | source)
XLA Modules:
  0.0 37.1 jit_solution(16682784567069760557)
XLA Ops:
  0.6 34.5 %solve.1 = (f32[4,84,512]{2,1,0:T(8,128)}, f32[16,128]{1,0:T(8,128)}) custom-call(f32[84,512]{1,0:T(8,128)} %b_ref.1, f32[84,512]{1,0:T(8,128)} %d_ref.1, f32[9,8,64,256]{3,2,1,0:T(8,128)} %k_hbm.1, s32[4,8]{1,0:T(4,128)} %bitcast.3, s32[1,2]{1,0:T(1,128)} %if_ref.1, s32[3,885]{1,0:T(4,128)} %bitcast.2, f32[885]{0:T(1024)} %val_ref.1), custom_call_target="tpu_custom_call" | custom-call | tf_op jit(solution)/shard_map/solve/pallas_call | solution.py:495
  35.2 1.9 %combine.1 = (f32[84,512]{1,0:T(8,128)}, f32[84,512]{1,0:T(8,128)}) custom-call(f32[4,84,512]{2,1,0:T(8,128)} %get-tuple-element.4.basis_ref, f32[16,128]{1,0:T(8,128)} %get-tuple-element.5.coef_ref), custom_call_target="tpu_custom_call" | custom-call | tf_op jit(solution)/shard_map/combine/pallas_call | solution.py:538

commit v7 on v6

--- a/solution.py
+++ b/solution.py
@@ -60,7 +60,7 @@
     n_space, n_chaos,
     b_ref, d_ref, k_hbm, col_ref, if_ref, tri_ref, val_ref,
     basis_out, coef_out,
-    kf, khi, klo, c3, cdiag, gb, gd, ef, vec, picked, rodd, reven,
+    kf, khi, klo, c2, cdiag, gb, gd, ef, vec, picked, rodd, reven,
     own_send, own_blocks, halo0, halo_out, halo_in, stat, red, natv,
     k_sem, gb_send, gb_recv, gd_send, gd_recv, h0_send, h0_recv, h_send, h_recv,
     r_send, r_recv,
@@ -208,9 +208,7 @@
             down = jnp.concatenate([down] * (depth // LANES), 1)
             hot.append(jnp.where(lanes_iota == down, 1.0, 0.0).astype(jnp.bfloat16))
         both = dot_nn(spread2, jnp.concatenate(hot, 0)).astype(jnp.bfloat16)
-        c3[parity, :, :depth] = both[:mp]
-        c3[parity, :, depth : 2 * depth] = both[mp:]
-        c3[parity, :, 2 * depth :] = both[:mp]
+        c2[parity] = both
 
     if depth > even_terms * mp:
         rest = jnp.zeros((depth - even_terms * mp, rodd.shape[2]), jnp.bfloat16)
@@ -310,9 +308,8 @@
                     k = half * per_half + i
                     hi, lo = picked[k, :, :wide], picked[k, :, wide:]
                     k_hi, k_lo = khi[k, :, start:stop], klo[k, :, start:stop]
-                    made.append(
-                        dot_nn(jnp.concatenate([hi, lo, hi], 1), jnp.concatenate([k_hi, k_hi, k_lo], 0))
-                    )
+                    both = dot_nn(jnp.concatenate([hi, lo], 0), k_hi)
+                    made.append(both[:mp] + both[mp:] + dot_nn(hi, k_lo))
                 for piece in range(start, stop, LANES):
                     tau = piece // LANES
                     a = made[0][:, piece - start : piece - start + LANES]
@@ -329,7 +326,8 @@
         coupled = []
         for parity, rhs in ((0, rodd), (1, reven)):
             hi, lo = rhs[0], rhs[1]
-            coupled.append(dot_nn(c3[parity], jnp.concatenate([hi, hi, lo], 0)))
+            both = dot_nn(c2[parity], hi)
+            coupled.append(both[:mp] + both[mp:] + dot_nn(c2[parity, :mp], lo))
 
         if it == 0:
             for d in range(1, n_chaos):
@@ -504,7 +502,7 @@
             pltpu.VMEM(stiffness.shape, f32),
             pltpu.VMEM((nbr, depth, cols), bf16),
             pltpu.VMEM((nbr, depth, cols), bf16),
-            pltpu.VMEM((2, mp, 3 * whole_depth), bf16),
+            pltpu.VMEM((2, 2 * mp, whole_depth), bf16),
             pltpu.VMEM((mp, LANES), f32),
             pltpu.VMEM((pairs, mp, LANES), f32),
             pltpu.VMEM((pairs, mp, LANES), f32),

time: 37.2 us -> 37.2 us (level)
  no operation moved by 1% of the time
where the time goes in v7:
time: 37.2 us; the launch traced here: 37 us
  Pallas kernels  36.4 us (98%)
  between operations  0.64 us (2%)
    pallas_call x1, Pallas kernels, per_device(): pl.pallas_call(functools.partial(kernel, n_space, n_chaos), out_shape=(ja...  34.5 us
    pallas_call x1, Pallas kernels, per_device(): pl.pallas_call(combine, out_shape=(out, out), in_specs=[vmem, vmem], out_...  1.93 us

profile of v7, /device:TPU:0, one launch (start us, length us, event | category | flops | bytes accessed | tf_op | source)
XLA Modules:
  0.0 37.0 jit_solution(7215632743410995589)
XLA Ops:
  0.6 34.5 %solve.1 = (f32[4,84,512]{2,1,0:T(8,128)}, f32[16,128]{1,0:T(8,128)}) custom-call(f32[84,512]{1,0:T(8,128)} %b_ref.1, f32[84,512]{1,0:T(8,128)} %d_ref.1, f32[9,8,64,256]{3,2,1,0:T(8,128)} %k_hbm.1, s32[4,8]{1,0:T(4,128)} %bitcast.3, s32[1,2]{1,0:T(1,128)} %if_ref.1, s32[3,885]{1,0:T(4,128)} %bitcast.2, f32[885]{0:T(1024)} %val_ref.1), custom_call_target="tpu_custom_call" | custom-call | tf_op jit(solution)/shard_map/solve/pallas_call | solution.py:493
  35.1 1.9 %combine.1 = (f32[84,512]{1,0:T(8,128)}, f32[84,512]{1,0:T(8,128)}) custom-call(f32[4,84,512]{2,1,0:T(8,128)} %get-tuple-element.4.basis_ref, f32[16,128]{1,0:T(8,128)} %get-tuple-element.5.coef_ref), custom_call_target="tpu_custom_call" | custom-call | tf_op jit(solution)/shard_map/combine/pallas_call | solution.py:536
